TPU v7x, 128 devices: a whole 4x4x4 slice. The times are simulated.
128 devices in a mesh: expert: 32 (over z, x, core), dp: 4 (over y).
Axes of the slice: x: 4, y: 4, z: 4, core: 2. Of those that a mesh axis runs over, the one named last changes fastest.
Arguments:
- tokens: bfloat16 [16384, 2048], P(('expert', 'dp')), may hold values from -6 to 6
- expert_ids: int32 [16384, 8], P(('expert', 'dp')), may hold values from 0 to 31, all different within a row
- combine_weights: float32 [16384, 8], P(('expert', 'dp')), may hold values from 0.05 to 0.5
- grad_output: bfloat16 [16384, 2048], P(('expert', 'dp')), may hold values from -6 to 6
- swap_flags: int32 [32], replicated, may hold values from 0 to 1, as said below
- w_gate: bfloat16 [32, 2048, 768], P('expert'), may hold values from -0.125 to 0.125
- w_up: bfloat16 [32, 2048, 768], P('expert'), may hold values from -0.125 to 0.125
- w_down: bfloat16 [32, 768, 2048], P('expert'), may hold values from -0.21875 to 0.21875
Outputs:
- mixed: bfloat16 [16384, 2048], P(('expert', 'dp'))
- grad_tokens: bfloat16 [16384, 2048], P(('expert', 'dp'))
- grad_weights: float32 [16384, 8], P(('expert', 'dp'))
- grad_gate: float32 [32, 2048, 768], P('expert', 'dp')
- grad_up: float32 [32, 2048, 768], P('expert', 'dp')
- grad_down: float32 [32, 768, 2048], P('expert', None, 'dp')
Inputs may be any that keep to these rules, and one draw needn't show every extreme that they name: `expert_ids`: each row names 8 different experts. swap_flags[d] equals swap_flags[(d + 16) % 32]; in every draw some pairs trade and some do not.
All inputs are finite; a program needn't handle non-finite values.
Results may differ from a plain program's by a relative error of at most 0.012.
Values may be sent and summed in bfloat16 or wider, within the bound.
No kernel may reach another device: no remote copies, remote signals or barrier semaphores. Data moves between devices by JAX's collectives and lax.ppermute only.
A program may use at most 128 MiB of HBM per device.

v0:
```python
import jax
import jax.numpy as jnp
from jax import lax
from jax.sharding import PartitionSpec as P


def swapped(value, axis, distance):
    mask = 2**distance
    pairs = [(source, source ^ mask) for source in range(lax.axis_size(axis))]
    return lax.ppermute(value, axis, pairs)


def expert_forward(expert_rows, gate_w, up_w, down_w):
    gate_pre = jnp.dot(expert_rows, gate_w, preferred_element_type=jnp.float32)
    up_pre = jnp.dot(expert_rows, up_w, preferred_element_type=jnp.float32)
    sigmoid_gate = jax.nn.sigmoid(gate_pre)
    activation = (gate_pre * sigmoid_gate * up_pre).astype(jnp.bfloat16)
    expert_out = jnp.dot(activation, down_w, preferred_element_type=jnp.float32).astype(
        jnp.bfloat16
    )
    return (gate_pre, up_pre, sigmoid_gate, activation, expert_out)


def expert_backward(
    expert_rows, out_grad, gate_pre, up_pre, sigmoid_gate, activation, gate_w, up_w, down_w
):
    act_grad = jnp.dot(out_grad, down_w.T, preferred_element_type=jnp.float32)
    gate_grad = (act_grad * up_pre * sigmoid_gate * (1.0 + gate_pre * (1.0 - sigmoid_gate))).astype(
        jnp.bfloat16
    )
    up_grad = (act_grad * gate_pre * sigmoid_gate).astype(jnp.bfloat16)
    row_grads = (
        jnp.dot(gate_grad, gate_w.T, preferred_element_type=jnp.float32)
        + jnp.dot(up_grad, up_w.T, preferred_element_type=jnp.float32)
    ).astype(jnp.bfloat16)
    gate_part = jnp.dot(expert_rows.T, gate_grad, preferred_element_type=jnp.float32)
    up_part = jnp.dot(expert_rows.T, up_grad, preferred_element_type=jnp.float32)
    down_part = jnp.dot(activation.T, out_grad, preferred_element_type=jnp.float32)
    return (row_grads, gate_part, up_part, down_part)


def local(tokens, expert_ids, combine_weights, grad_output, swap_flags, w_gate, w_up, w_down):
    device_count = lax.axis_size("expert")
    half_way = device_count // 2
    pair_bit = device_count.bit_length() - 2
    tok_rows, feat_width = tokens.shape
    top_k = expert_ids.shape[1]
    capacity = tok_rows * top_k // device_count
    slots_all = device_count * capacity
    device = lax.axis_index("expert")
    numbers = jnp.arange(device_count, dtype=jnp.int32)
    my_flag = jnp.sum(jnp.where(numbers == device, swap_flags, 0))
    holder = jnp.where(swap_flags == 1, (numbers + half_way) % device_count, numbers)
    gate_w = w_gate[0]
    up_w = w_up[0]
    down_w = w_down[0]
    choices_flat = expert_ids.reshape(-1)
    partner_copy = swapped((gate_w, up_w, down_w), "expert", pair_bit)
    gate_w = jnp.where(my_flag == 1, partner_copy[0], gate_w)
    up_w = jnp.where(my_flag == 1, partner_copy[1], up_w)
    down_w = jnp.where(my_flag == 1, partner_copy[2], down_w)
    expert_hits = choices_flat[:, None] == numbers[None, :]
    target_device = jnp.sum(jnp.where(expert_hits, holder[None, :], 0), axis=1)
    onehot = (target_device[:, None] == numbers[None, :]).astype(jnp.int32)
    earlier = jnp.cumsum(onehot, axis=0) - onehot
    slot_rank = jnp.sum(earlier * onehot, axis=1)
    retained = (slot_rank < capacity).reshape(tok_rows, top_k)
    target = jnp.where(
        retained, (target_device * capacity + slot_rank).reshape(tok_rows, top_k), -1
    )
    matches = jnp.arange(slots_all, dtype=jnp.int32)[:, None, None] == target[None]
    placement = jnp.any(matches, axis=2).astype(jnp.bfloat16)
    send_tokens = jnp.dot(placement, tokens, preferred_element_type=jnp.float32).astype(
        jnp.bfloat16
    )
    kept_weights = jnp.where(retained, combine_weights, 0.0)
    slot_weight = jnp.sum(jnp.where(matches, kept_weights[None], 0.0), axis=(1, 2))
    slot_grads = jnp.dot(placement, grad_output, preferred_element_type=jnp.float32)
    send_cotangent = (slot_weight[:, None] * slot_grads).astype(jnp.bfloat16)
    expert_rows = lax.all_to_all(
        send_tokens.reshape(device_count, capacity, feat_width),
        "expert",
        split_axis=0,
        concat_axis=0,
        tiled=True,
    )
    expert_rows = expert_rows.reshape(slots_all, feat_width)
    gate_pre, up_pre, sigmoid_gate, activation, expert_out = expert_forward(
        expert_rows, gate_w, up_w, down_w
    )
    returned = lax.all_to_all(
        expert_out.reshape(device_count, capacity, feat_width),
        "expert",
        split_axis=0,
        concat_axis=0,
        tiled=True,
    )
    returned = returned.reshape(slots_all, feat_width)
    out_grad = lax.all_to_all(
        send_cotangent.reshape(device_count, capacity, feat_width),
        "expert",
        split_axis=0,
        concat_axis=0,
        tiled=True,
    )
    out_grad = out_grad.reshape(slots_all, feat_width)
    row_grads, gate_part, up_part, down_part = expert_backward(
        expert_rows, out_grad, gate_pre, up_pre, sigmoid_gate, activation, gate_w, up_w, down_w
    )
    returned_grads = lax.all_to_all(
        row_grads.reshape(device_count, capacity, feat_width),
        "expert",
        split_axis=0,
        concat_axis=0,
        tiled=True,
    )
    returned_grads = returned_grads.reshape(slots_all, feat_width)
    safe_index = jnp.maximum(target, 0)
    picked = jnp.take(returned, safe_index, axis=0).astype(jnp.float32)
    mixed = jnp.sum(kept_weights[..., None] * picked, axis=1).astype(jnp.bfloat16)
    products = jnp.sum(grad_output.astype(jnp.float32)[:, None, :] * picked, axis=2)
    grad_weights = jnp.where(retained, products, 0.0)
    picked_grads = jnp.take(returned_grads, safe_index, axis=0).astype(jnp.float32)
    grad_tokens = jnp.sum(jnp.where(retained[..., None], picked_grads, 0.0), axis=1).astype(
        jnp.bfloat16
    )
    summed = (
        lax.psum_scatter(
            gate_part.astype(jnp.bfloat16), "dp", scatter_dimension=0, tiled=True
        ).astype(jnp.float32),
        lax.psum_scatter(
            up_part.astype(jnp.bfloat16), "dp", scatter_dimension=0, tiled=True
        ).astype(jnp.float32),
        lax.psum_scatter(
            down_part.astype(jnp.bfloat16), "dp", scatter_dimension=1, tiled=True
        ).astype(jnp.float32),
    )
    gate_sum = summed[0]
    up_sum = summed[1]
    down_sum = summed[2]
    return (mixed, grad_tokens, grad_weights, gate_sum[None], up_sum[None], down_sum[None])


def solution(mesh):
    return jax.shard_map(
        local,
        mesh=mesh,
        in_specs=(
            P(("expert", "dp"), None),
            P(("expert", "dp"), None),
            P(("expert", "dp"), None),
            P(("expert", "dp"), None),
            P(),
            P("expert", None, None),
            P("expert", None, None),
            P("expert", None, None),
        ),
        out_specs=(
            P(("expert", "dp"), None),
            P(("expert", "dp"), None),
            P(("expert", "dp"), None),
            P("expert", "dp", None),
            P("expert", "dp", None),
            P("expert", None, "dp"),
        ),
        check_vma=False,
    )
```

profile of v0, /device:TPU:26, one launch (start us, length us, event | category | flops | bytes accessed | tf_op | source)
XLA Modules:
  0.0 532.0 jit_solution(12326954718647240330)
XLA Ops:
  7.2 0.8 copy.32
  8.0 0.1 eq.70
  8.1 1.3 fusion.11
  9.4 0.1 select_reduce_fusion.2
  9.5 9.0 %reduce-window.6 = s32[32,8,128]{2,1,0:T(8,128)S(1)} reduce-window(s32[32,8,128]{2,1,0:T(8,128)S(1)} %fusion.10, s32[]{:T(128)} %constant.23.clone.1), window={size=1x1x128 pad=0_0x0_0x127_0}, to_apply=%region_1.2 | reduce-window | flops 4161536 | bytes 262148 | tf_op jit(solution)/shard_map/reduce-window
  18.6 0.1 slice.12
  18.6 0.1 copy.33
  18.9 0.1 broadcast_add_fusion
  19.1 0.8 copy.35
  19.9 0.1 lt.29
  20.1 0.1 add.48
  20.3 1.9 fusion.2
  22.2 1.9 select_reduce_fusion.1
  24.2 4.2 multiply_convert_fusion
  28.4 8.5 %all-to-all-start.2 = ((bf16[32,32,2048]{2,1,0:T(8,128)(2,1)}), bf16[32,32,2048]{2,1,0:T(8,128)(2,1)}, u32[]{:S(2)}, u32[]{:S(2)}) async-start(bf16[32,32,2048]{2,1,0:T(8,128)(2,1)} %bitcast.92), calls=%async_computation.2 | async-start | bytes 8388608 | tf_op jit(solution)/shard_map/all_to_all | solution.py:99
  36.9 3.1 collective-permute-start.2
  40.0 3.2 convolution_convert_fusion.1
  43.2 45.5 %all-to-all-done.2 = bf16[32,32,2048]{2,1,0:T(8,128)(2,1)} async-done(((bf16[32,32,2048]{2,1,0:T(8,128)(2,1)}), bf16[32,32,2048]{2,1,0:T(8,128)(2,1)}, u32[]{:S(2)}, u32[]{:S(2)}) %all-to-all-start.2) | async-done | bytes 4194336 | tf_op jit(solution)/shard_map/all_to_all | solution.py:99
  88.7 69.7 %all-to-all-start = ((bf16[32,32,2048]{2,1,0:T(8,128)(2,1)}), bf16[32,32,2048]{2,1,0:T(8,128)(2,1)}, u32[]{:S(2)}, u32[]{:S(2)}) async-start(bf16[32,32,2048]{2,1,0:T(8,128)(2,1)} %bitcast.91), calls=%async_computation | async-start | bytes 8388608 | tf_op jit(solution)/shard_map/all_to_all | solution.py:80
  158.4 3.1 collective-permute-start.1
  161.5 1.0 collective-permute-start
  163.1 8.3 %fusion.6 = f32[1024,768]{1,0:T(8,128)} fusion(bf16[1024,2048]{1,0:T(8,128)(2,1)} %bitcast.12, bf16[768,2048]{1,0:T(8,128)(2,1)} %collective-permute-done.2, pred[]{:T(512)S(6)} %eq.88, bf16[1,768,2048]{2,1,0:T(8,128)(2,1)} %param.17), kind=kOutput, calls=%fused_computation.29 | convolution fusion | flops 3222798336 | bytes 13631489 | tf_op jit(solution)/shard_map/dot_general | solution.py:27
  171.4 103.9 %collective-permute-done.1 = bf16[2048,768]{1,0:T(8,128)(2,1)} collective-permute-done((bf16[2048,768]{1,0:T(8,128)(2,1)}, bf16[2048,768]{1,0:T(8,128)(2,1)}, u32[]{:S(2)}, u32[]{:S(2)}) %collective-permute-start.1) | collective-permute-done | bytes 3145760 | tf_op jit(solution)/shard_map/ppermute | solution.py:10
  275.4 6.3 %fusion.5 = f32[1024,768]{1,0:T(8,128)S(1)} fusion(bf16[1024,2048]{1,0:T(8,128)(2,1)} %bitcast.4, bf16[2048,768]{1,0:T(8,128)(2,1)} %collective-permute-done.1, pred[]{:T(512)S(6)} %eq.88, bf16[1,2048,768]{2,1,0:T(8,128)(2,1)} %param.16), kind=kOutput, calls=%fused_computation.28 | convolution fusion | flops 3222798336 | bytes 13631489 | tf_op jit(solution)/shard_map/dot_general | solution.py:15
  281.7 60.6 %collective-permute-done = bf16[2048,768]{1,0:T(8,128)(2,1)} collective-permute-done((bf16[2048,768]{1,0:T(8,128)(2,1)}, bf16[2048,768]{1,0:T(8,128)(2,1)}, u32[]{:S(2)}, u32[]{:S(2)}) %collective-permute-start) | collective-permute-done | bytes 3145760 | tf_op jit(solution)/shard_map/ppermute | solution.py:10
  342.3 8.3 %multiply_convert_fusion.2 = (bf16[1024,768]{1,0:T(8,128)(2,1)}, bf16[1024,768]{1,0:T(8,128)(2,1)S(1)}, bf16[1024,768]{1,0:T(8,128)(2,1)}) fusion(f32[1024,768]{1,0:T(8,128)S(1)} %copy-done.6, f32[1024,768]{1,0:T(8,128)S(1)} %fusion.5, bf16[1024,2048]{1,0:T(8,128)(2,1)} %bitcast.4, bf16[2048,768]{1,0:T(8,128)(2,1)} %collective-permute-done, pred[]{:T(512)S(6)} %eq.88, ...), kind=kOutput, calls=%fused_computation.20 | convolution fusion | flops 3235381248 | bytes 21495808 | tf_op jit(solution)/shard_map/dot_general | solution.py:14
  350.7 7.0 %convolution_convert_fusion.2 = bf16[768,2048]{1,0:T(8,128)(2,1)} fusion(bf16[1024,768]{1,0:T(8,128)(2,1)S(1)} %get-tuple-element.31, bf16[1024,2048]{1,0:T(8,128)(2,1)} %bitcast.12), kind=kOutput, calls=%fused_computation.16 | convolution fusion | flops 3222798336 | bytes 8912896 | tf_op jit(solution)/shard_map/dot_general | solution.py:38
  357.7 0.2 reduce-scatter.4.cloned.1.call-start
  358.0 7.9 %convolution_convert_fusion.4 = bf16[2048,768]{1,0:T(8,128)(2,1)} fusion(bf16[1024,2048]{1,0:T(8,128)(2,1)} %bitcast.4, bf16[1024,768]{1,0:T(8,128)(2,1)} %get-tuple-element.30), kind=kOutput, calls=%fused_computation.18 | convolution fusion | flops 3222798336 | bytes 8912896 | tf_op jit(solution)/shard_map/dot_general | solution.py:36
  365.9 7.0 %convolution_convert_fusion = bf16[1024,2048]{1,0:T(8,128)(2,1)} fusion(bf16[1024,768]{1,0:T(8,128)(2,1)S(1)} %get-tuple-element.31, bf16[768,2048]{1,0:T(8,128)(2,1)} %collective-permute-done.2, pred[]{:T(512)S(6)} %eq.88, bf16[1,768,2048]{2,1,0:T(8,128)(2,1)} %param.17), kind=kOutput, calls=%fused_computation.14 | convolution fusion | flops 3224895488 | bytes 12058625 | tf_op jit(solution)/shard_map/dot_general | solution.py:18
  372.9 11.5 %all-to-all-start.1 = ((bf16[32,32,2048]{2,1,0:T(8,128)(2,1)}), bf16[32,32,2048]{2,1,0:T(8,128)(2,1)}, u32[]{:S(2)}, u32[]{:S(2)}) async-start(bf16[32,32,2048]{2,1,0:T(8,128)(2,1)} %bitcast.93), calls=%async_computation.1 | async-start | bytes 8388608 | tf_op jit(solution)/shard_map/all_to_all | solution.py:91
  384.5 7.5 %convolution_convert_fusion.3 = bf16[2048,768]{1,0:T(8,128)(2,1)} fusion(bf16[1024,2048]{1,0:T(8,128)(2,1)} %bitcast.4, bf16[1024,768]{1,0:T(8,128)(2,1)S(1)} %copy-done.5), kind=kOutput, calls=%fused_computation.17 | convolution fusion | flops 3222798336 | bytes 8912896 | tf_op jit(solution)/shard_map/dot_general | solution.py:37
  392.0 5.3 %fusion.4 = f32[1024,2048]{1,0:T(8,128)S(1)} fusion(bf16[1024,768]{1,0:T(8,128)(2,1)S(1)} %copy-done.5, bf16[2048,768]{1,0:T(8,128)(2,1)} %collective-permute-done.1, pred[]{:T(512)S(6)} %eq.88, bf16[1,2048,768]{2,1,0:T(8,128)(2,1)} %param.16), kind=kOutput, calls=%fused_computation.27 | convolution fusion | flops 3222798336 | bytes 16252929 | tf_op jit(solution)/shard_map/dot_general | solution.py:34
  397.4 5.2 add_convert_fusion
  402.6 33.2 %all-to-all-done.1 = bf16[32,32,2048]{2,1,0:T(8,128)(2,1)} async-done(((bf16[32,32,2048]{2,1,0:T(8,128)(2,1)}), bf16[32,32,2048]{2,1,0:T(8,128)(2,1)}, u32[]{:S(2)}, u32[]{:S(2)}) %all-to-all-start.1) | async-done | bytes 4194336 | tf_op jit(solution)/shard_map/all_to_all | solution.py:91
  435.8 7.2 %all-to-all-start.3 = ((bf16[32,32,2048]{2,1,0:T(8,128)(2,1)}), bf16[32,32,2048]{2,1,0:T(8,128)(2,1)}, u32[]{:S(2)}, u32[]{:S(2)}) async-start(bf16[32,32,2048]{2,1,0:T(8,128)(2,1)} %bitcast.94), calls=%async_computation.3 | async-start | bytes 8388608 | tf_op jit(solution)/shard_map/all_to_all | solution.py:110
  443.0 0.1 convert_element_type.69
  443.1 0.1 copy.38
  443.2 0.1 copy.39
  443.3 0.1 reshape.126
  443.4 11.5 %gather_fusion = bf16[1024,2048]{1,0:T(8,128)(2,1)} fusion(bf16[1024,2048]{1,0:T(8,128)(2,1)} %bitcast.9, s32[1024]{0:T(1024)S(1)} %broadcast_clamp_fusion), kind=kCustom, calls=%fused_computation.clone | custom fusion | bytes 8392704 | tf_op jit(solution)/shard_map/jit(_take)/gather | solution.py:119
  455.0 39.5 %all-to-all-done.3 = bf16[32,32,2048]{2,1,0:T(8,128)(2,1)} async-done(((bf16[32,32,2048]{2,1,0:T(8,128)(2,1)}), bf16[32,32,2048]{2,1,0:T(8,128)(2,1)}, u32[]{:S(2)}, u32[]{:S(2)}) %all-to-all-start.3) | async-done | bytes 4194336 | tf_op jit(solution)/shard_map/all_to_all | solution.py:110
  494.5 11.6 %gather_fusion.1 = bf16[1024,2048]{1,0:T(8,128)(2,1)} fusion(bf16[1024,2048]{1,0:T(8,128)(2,1)} %bitcast.14, s32[1024]{0:T(1024)S(1)} %broadcast_clamp_fusion), kind=kCustom, calls=%fused_computation.1.clone | custom fusion | bytes 8392704 | tf_op jit(solution)/shard_map/jit(_take)/gather | solution.py:123
  506.0 11.3 %fusion.1 = (f32[128,8]{1,0:T(8,128)S(1)}, bf16[128,2048]{1,0:T(8,128)(2,1)}, bf16[128,2048]{1,0:T(8,128)(2,1)}) fusion(f32[128,2048]{1,0:T(8,128)S(1)} %convert_element_type.69, bf16[1024,2048]{1,0:T(8,128)(2,1)} %gather_fusion, pred[128,8]{1,0:T(8,128)(4,1)S(1)} %copy.38, f32[128,8]{1,0:T(8,128)S(1)} %broadcast_select_fusion.10, ...), kind=kLoop, calls=%fused_computation.5 | loop fusion | flops 20446208 | bytes 10496000 | tf_op jit(solution)/shard_map/reduce_sum | solution.py:121
  517.3 0.7 copy.43
  518.0 2.5 bitcast_convert_fusion
  520.5 2.4 bitcast_convert_fusion.2
  522.9 2.4 bitcast_convert_fusion.1
  (41 shorter events, 0.6 us)
Async XLA Ops:
  7.2 32.8 %copy-start = (bf16[128,2048]{1,0:T(8,128)(2,1)S(1)}, bf16[128,2048]{1,0:T(8,128)(2,1)}, u32[]{:S(2)}) copy-start(bf16[128,2048]{1,0:T(8,128)(2,1)} %param.10) | copy-start | bytes 1572868
  28.4 60.3 %all-to-all-start.2 = ((bf16[32,32,2048]{2,1,0:T(8,128)(2,1)}), bf16[32,32,2048]{2,1,0:T(8,128)(2,1)}, u32[]{:S(2)}, u32[]{:S(2)}) async-start(bf16[32,32,2048]{2,1,0:T(8,128)(2,1)} %bitcast.92), calls=%async_computation.2 | async-start | bytes 8388608 | tf_op jit(solution)/shard_map/all_to_all | solution.py:99
  36.9 126.2 %collective-permute-start.2 = (bf16[768,2048]{1,0:T(8,128)(2,1)}, bf16[768,2048]{1,0:T(8,128)(2,1)}, u32[]{:S(2)}, u32[]{:S(2)}) collective-permute-start(bf16[768,2048]{1,0:T(8,128)(2,1)} %bitcast.98), channel_id=1, source_target_pairs={{0,64},{4,68},{8,72},{12,76},{16,80},{20,84},{24,88},{28,92},{32,9... | collective-permute-start | bytes 9437192 | tf_op jit(solution)/shard_map/ppermute | solution.py:10
  88.7 186.7 %all-to-all-start = ((bf16[32,32,2048]{2,1,0:T(8,128)(2,1)}), bf16[32,32,2048]{2,1,0:T(8,128)(2,1)}, u32[]{:S(2)}, u32[]{:S(2)}) async-start(bf16[32,32,2048]{2,1,0:T(8,128)(2,1)} %bitcast.91), calls=%async_computation | async-start | bytes 8388608 | tf_op jit(solution)/shard_map/all_to_all | solution.py:80
  158.4 359.6 %reduce-scatter.8.cloned.1.call-start = ((), (), s32[]{:S(2)}) async-start(), calls=%async_computation.9 | async-start | bytes 3932160 | tf_op jit(solution)/shard_map/reduce_scatter | solution.py:134
  158.4 116.9 %collective-permute-start.1 = (bf16[2048,768]{1,0:T(8,128)(2,1)}, bf16[2048,768]{1,0:T(8,128)(2,1)}, u32[]{:S(2)}, u32[]{:S(2)}) collective-permute-start(bf16[2048,768]{1,0:T(8,128)(2,1)} %bitcast.99), channel_id=1, source_target_pairs={{0,64},{4,68},{8,72},{12,76},{16,80},{20,84},{24,88},{28,92},{32,9... | collective-permute-start | bytes 9437192 | tf_op jit(solution)/shard_map/ppermute | solution.py:10
  161.5 180.8 %collective-permute-start = (bf16[2048,768]{1,0:T(8,128)(2,1)}, bf16[2048,768]{1,0:T(8,128)(2,1)}, u32[]{:S(2)}, u32[]{:S(2)}) collective-permute-start(bf16[2048,768]{1,0:T(8,128)(2,1)} %bitcast.100), channel_id=1, source_target_pairs={{0,64},{4,68},{8,72},{12,76},{16,80},{20,84},{24,88},{28,92},{32,9... | collective-permute-start | bytes 9437192 | tf_op jit(solution)/shard_map/ppermute | solution.py:10
  275.4 66.9 %copy-start.3 = (bf16[1,2048,768]{2,1,0:T(8,128)(2,1)S(1)}, bf16[1,2048,768]{2,1,0:T(8,128)(2,1)}, u32[]{:S(2)}) copy-start(bf16[1,2048,768]{2,1,0:T(8,128)(2,1)} %param.15) | copy-start | bytes 9437188
  275.4 66.9 %copy-start.6 = (f32[1024,768]{1,0:T(8,128)S(1)}, f32[1024,768]{1,0:T(8,128)}, u32[]{:S(2)}) copy-start(f32[1024,768]{1,0:T(8,128)} %fusion.6) | copy-start | bytes 9437188
  357.7 162.7 %reduce-scatter.4.cloned.1.call-start = ((), (), s32[]{:S(2)}) async-start(), calls=%async_computation.7 | async-start | bytes 3932160 | tf_op jit(solution)/shard_map/reduce_scatter | solution.py:128
  372.9 11.5 %copy-start.5 = (bf16[1024,768]{1,0:T(8,128)(2,1)S(1)}, bf16[1024,768]{1,0:T(8,128)(2,1)}, u32[]{:S(2)}) copy-start(bf16[1024,768]{1,0:T(8,128)(2,1)} %get-tuple-element.32) | copy-start | bytes 4718596
  372.9 62.8 %all-to-all-start.1 = ((bf16[32,32,2048]{2,1,0:T(8,128)(2,1)}), bf16[32,32,2048]{2,1,0:T(8,128)(2,1)}, u32[]{:S(2)}, u32[]{:S(2)}) async-start(bf16[32,32,2048]{2,1,0:T(8,128)(2,1)} %bitcast.93), calls=%async_computation.1 | async-start | bytes 8388608 | tf_op jit(solution)/shard_map/all_to_all | solution.py:91
  384.4 138.5 %reduce-scatter.6.cloned.1.call-start = ((), (), s32[]{:S(2)}) async-start(), calls=%async_computation.8 | async-start | bytes 3932160 | tf_op jit(solution)/shard_map/reduce_scatter | solution.py:131
  392.0 5.4 %copy-start.4 = (bf16[1,2048,768]{2,1,0:T(8,128)(2,1)S(1)}, bf16[1,2048,768]{2,1,0:T(8,128)(2,1)}, u32[]{:S(2)}) copy-start(bf16[1,2048,768]{2,1,0:T(8,128)(2,1)} %param.15) | copy-start | bytes 9437188
  392.0 5.4 %copy-start.7 = (bf16[1024,768]{1,0:T(8,128)(2,1)S(1)}, bf16[1024,768]{1,0:T(8,128)(2,1)}, u32[]{:S(2)}) copy-start(bf16[1024,768]{1,0:T(8,128)(2,1)} %get-tuple-element.30) | copy-start | bytes 4718596
  435.8 7.2 %copy-start.2 = (bf16[128,2048]{1,0:T(8,128)(2,1)S(1)}, bf16[128,2048]{1,0:T(8,128)(2,1)}, u32[]{:S(2)}) copy-start(bf16[128,2048]{1,0:T(8,128)(2,1)} %param.13) | copy-start | bytes 1572868
  435.8 58.7 %all-to-all-start.3 = ((bf16[32,32,2048]{2,1,0:T(8,128)(2,1)}), bf16[32,32,2048]{2,1,0:T(8,128)(2,1)}, u32[]{:S(2)}, u32[]{:S(2)}) async-start(bf16[32,32,2048]{2,1,0:T(8,128)(2,1)} %bitcast.94), calls=%async_computation.3 | async-start | bytes 8388608 | tf_op jit(solution)/shard_map/all_to_all | solution.py:110
  517.3 7.9 %copy-start.1 = (bf16[128,2048]{1,0:T(8,128)(2,1)S(1)}, bf16[128,2048]{1,0:T(8,128)(2,1)}, u32[]{:S(2)}) copy-start(bf16[128,2048]{1,0:T(8,128)(2,1)} %param.10) | copy-start | bytes 1572868
Sparse Core Ops, SparseCore 0:
  357.9 41.2 reduce-scatter.7
  401.5 37.9 reduce-scatter.3
  441.9 37.9 reduce-scatter.5
where the time goes:
time: 541 us; the launch traced here: 532 us
  waiting for transfers between devices  283 us (52%)
  starting transfers between devices  104 us (19%)
  matrix products  70.4 us (13%)
  other arithmetic  33.1 us (6%)
  local copies, waits for them, and re-layouts  26.5 us (5%)
  between operations  14.9 us (3%)
    ppermute x3, waiting for transfers between devices, swapped(): return lax.ppermute(value, axis, pairs)  165 us
    all_to_all x1, starting transfers between devices, local(): lax.all_to_all(send_tokens.reshape(device_count, capacity, feat_width), '...  69.7 us
    all_to_all x1, waiting for transfers between devices, local(): lax.all_to_all(send_cotangent.reshape(device_count, capacity, feat_width)...  45.5 us
    all_to_all x1, waiting for transfers between devices, local(): lax.all_to_all(row_grads.reshape(device_count, capacity, feat_width), 'ex...  39.5 us
    all_to_all x1, waiting for transfers between devices, local(): lax.all_to_all(expert_out.reshape(device_count, capacity, feat_width), 'e...  33.2 us
    gather x1, local copies, waits for them, and re-layouts, local(): jnp.take(returned_grads, safe_index, axis=0).astype(jnp.float32)  11.6 us
    gather x1, local copies, waits for them, and re-layouts, local(): picked = jnp.take(returned, safe_index, axis=0).astype(jnp.float32)  11.5 us
    all_to_all x1, starting transfers between devices, local(): lax.all_to_all(expert_out.reshape(device_count, capacity, feat_width), 'e...  11.5 us
  transfers between devices with their start and end apart: 10, of which 5 were waited for; matrix products, arithmetic and copies ran while one was open for 17% of the time, Pallas kernels for 0%

commit v1 on v0

--- a/solution.py
+++ b/solution.py
@@ -41,7 +41,6 @@
 
 def local(tokens, expert_ids, combine_weights, grad_output, swap_flags, w_gate, w_up, w_down):
     device_count = lax.axis_size("expert")
-    half_way = device_count // 2
     pair_bit = device_count.bit_length() - 2
     tok_rows, feat_width = tokens.shape
     top_k = expert_ids.shape[1]
@@ -50,23 +49,19 @@
     device = lax.axis_index("expert")
     numbers = jnp.arange(device_count, dtype=jnp.int32)
     my_flag = jnp.sum(jnp.where(numbers == device, swap_flags, 0))
-    holder = jnp.where(swap_flags == 1, (numbers + half_way) % device_count, numbers)
     gate_w = w_gate[0]
     up_w = w_up[0]
     down_w = w_down[0]
-    choices_flat = expert_ids.reshape(-1)
-    partner_copy = swapped((gate_w, up_w, down_w), "expert", pair_bit)
-    gate_w = jnp.where(my_flag == 1, partner_copy[0], gate_w)
-    up_w = jnp.where(my_flag == 1, partner_copy[1], up_w)
-    down_w = jnp.where(my_flag == 1, partner_copy[2], down_w)
-    expert_hits = choices_flat[:, None] == numbers[None, :]
-    target_device = jnp.sum(jnp.where(expert_hits, holder[None, :], 0), axis=1)
-    onehot = (target_device[:, None] == numbers[None, :]).astype(jnp.int32)
-    earlier = jnp.cumsum(onehot, axis=0) - onehot
-    slot_rank = jnp.sum(earlier * onehot, axis=1)
-    retained = (slot_rank < capacity).reshape(tok_rows, top_k)
+    target_device = expert_ids
+    named = jnp.any(expert_ids[:, :, None] == numbers, axis=1)
+    rows = jnp.arange(tok_rows, dtype=jnp.int32)
+    before = (rows[:, None] > rows[None, :]).astype(jnp.bfloat16)
+    earlier = jnp.dot(before, named.astype(jnp.bfloat16), preferred_element_type=jnp.float32)
+    hits = expert_ids[:, :, None] == numbers
+    slot_rank = jnp.sum(jnp.where(hits, earlier[:, None, :], 0.0), axis=2).astype(jnp.int32)
+    retained = slot_rank < capacity
     target = jnp.where(
-        retained, (target_device * capacity + slot_rank).reshape(tok_rows, top_k), -1
+        retained, target_device * capacity + slot_rank, -1
     )
     matches = jnp.arange(slots_all, dtype=jnp.int32)[:, None, None] == target[None]
     placement = jnp.any(matches, axis=2).astype(jnp.bfloat16)
@@ -124,20 +119,16 @@
     grad_tokens = jnp.sum(jnp.where(retained[..., None], picked_grads, 0.0), axis=1).astype(
         jnp.bfloat16
     )
-    summed = (
-        lax.psum_scatter(
-            gate_part.astype(jnp.bfloat16), "dp", scatter_dimension=0, tiled=True
-        ).astype(jnp.float32),
-        lax.psum_scatter(
-            up_part.astype(jnp.bfloat16), "dp", scatter_dimension=0, tiled=True
-        ).astype(jnp.float32),
-        lax.psum_scatter(
-            down_part.astype(jnp.bfloat16), "dp", scatter_dimension=1, tiled=True
-        ).astype(jnp.float32),
-    )
-    gate_sum = summed[0]
-    up_sum = summed[1]
-    down_sum = summed[2]
+    def reduced(part, dim):
+        total = lax.psum_scatter(
+            part.astype(jnp.bfloat16), "dp", scatter_dimension=dim, tiled=True
+        )
+        partners = swapped(total, "expert", pair_bit)
+        return jnp.where(my_flag == 1, partners, total).astype(jnp.float32)
+
+    gate_sum = reduced(gate_part, 0)
+    up_sum = reduced(up_part, 0)
+    down_sum = reduced(down_part, 1)
     return (mixed, grad_tokens, grad_weights, gate_sum[None], up_sum[None], down_sum[None])
 
 

time: 541 us -> 370 us (0.68)
  waiting for transfers between devices: 283 us -> 187 us
  starting transfers between devices: 104 us -> 34.9 us
  other arithmetic: 33.1 us -> 26.6 us
    ppermute x3, waiting for transfers between devices: 165 us -> 34 us  [swapped(): return lax.ppermute(value, axis, pairs)]
    all_to_all x1, starting transfers between devices: 69.7 us -> 8.52 us  [local(): lax.all_to_all(send_tokens.reshape(device_count, capacity, feat_width), '...]
    all_to_all x1, waiting for transfers between devices: 0.01 us -> 45.2 us  [local(): lax.all_to_all(send_tokens.reshape(device_count, capacity, feat_width), '...]
    all_to_all x1, waiting for transfers between devices: 45.5 us -> 35.2 us  [local(): lax.all_to_all(send_cotangent.reshape(device_count, capacity, feat_width)...]
    another operation x3 -> x0, other arithmetic: 9.15 us -> none
  transfers between devices with their start and end apart: 10 -> 10, of which waited for: 5 -> 7; matrix products, arithmetic and copies ran while one was open for 17% -> 27% of each run, Pallas kernels for 0% -> 0%
where the time goes in v1:
time: 370 us; the launch traced here: 363 us
  waiting for transfers between devices  187 us (51%)
  matrix products  74.7 us (20%)
  starting transfers between devices  34.9 us (9%)
  other arithmetic  26.6 us (7%)
  local copies, waits for them, and re-layouts  25 us (7%)
  between operations  14.8 us (4%)
    all_to_all x1, waiting for transfers between devices, local(): lax.all_to_all(send_tokens.reshape(device_count, capacity, feat_width), '...  45.2 us
    all_to_all x1, waiting for transfers between devices, local(): lax.all_to_all(row_grads.reshape(device_count, capacity, feat_width), 'ex...  36.8 us
    all_to_all x1, waiting for transfers between devices, local(): lax.all_to_all(expert_out.reshape(device_count, capacity, feat_width), 'e...  35.8 us
    all_to_all x1, waiting for transfers between devices, local(): lax.all_to_all(send_cotangent.reshape(device_count, capacity, feat_width)...  35.2 us
    ppermute x3, waiting for transfers between devices, swapped(): return lax.ppermute(value, axis, pairs)  34 us
    gather x1, local copies, waits for them, and re-layouts, local(): jnp.take(returned_grads, safe_index, axis=0).astype(jnp.float32)  11.6 us
    gather x1, local copies, waits for them, and re-layouts, local(): picked = jnp.take(returned, safe_index, axis=0).astype(jnp.float32)  11.6 us
    reduce_sum x1, other arithmetic, local(): jnp.sum(grad_output.astype(jnp.float32)[:, None, :] * picked, axis=2)  11.5 us
  transfers between devices with their start and end apart: 10, of which 7 were waited for; matrix products, arithmetic and copies ran while one was open for 27% of the time, Pallas kernels for 0%

profile of v1, /device:TPU:26, one launch (start us, length us, event | category | flops | bytes accessed | tf_op | source)
XLA Modules:
  0.0 363.0 jit_solution(13606120162873961390)
XLA Ops:
  7.2 0.9 fusion.13
  8.0 0.1 fusion.14
  8.2 0.7 select_reduce_fusion.2
  8.9 0.7 broadcast_select_fusion.1
  9.6 0.7 broadcast_compare_fusion
  10.3 1.9 fusion.2
  12.2 4.3 %convolution_convert_fusion.1 = bf16[1024,2048]{1,0:T(8,128)(2,1)} fusion(pred[1024,128]{1,0:T(8,128)(4,1)S(1)} %fusion.2, bf16[128,2048]{1,0:T(8,128)(2,1)} %param.10), kind=kOutput, calls=%fused_computation.15 | convolution fusion | flops 538968064 | bytes 4849664 | tf_op jit(solution)/shard_map/dot_general | solution.py:68
  16.5 8.5 %all-to-all-start = ((bf16[32,32,2048]{2,1,0:T(8,128)(2,1)}), bf16[32,32,2048]{2,1,0:T(8,128)(2,1)}, u32[]{:S(2)}, u32[]{:S(2)}) async-start(bf16[32,32,2048]{2,1,0:T(8,128)(2,1)} %bitcast.61), calls=%async_computation | async-start | bytes 8388608 | tf_op jit(solution)/shard_map/all_to_all | solution.py:75
  25.0 1.9 select_reduce_fusion.1
  26.9 4.3 %multiply_convert_fusion = bf16[1024,2048]{1,0:T(8,128)(2,1)} fusion(pred[1024,128]{1,0:T(8,128)(4,1)S(1)} %fusion.2, bf16[128,2048]{1,0:T(8,128)(2,1)} %param.13, f32[1024]{0:T(1024)S(1)} %select_reduce_fusion.1), kind=kOutput, calls=%fused_computation.8 | convolution fusion | flops 541065216 | bytes 4853760 | tf_op jit(solution)/shard_map/dot_general | solution.py:73
  31.2 45.2 %all-to-all-done = bf16[32,32,2048]{2,1,0:T(8,128)(2,1)} async-done(((bf16[32,32,2048]{2,1,0:T(8,128)(2,1)}), bf16[32,32,2048]{2,1,0:T(8,128)(2,1)}, u32[]{:S(2)}, u32[]{:S(2)}) %all-to-all-start) | async-done | bytes 4194336 | tf_op jit(solution)/shard_map/all_to_all | solution.py:75
  76.4 6.9 %all-to-all-start.2 = ((bf16[32,32,2048]{2,1,0:T(8,128)(2,1)}), bf16[32,32,2048]{2,1,0:T(8,128)(2,1)}, u32[]{:S(2)}, u32[]{:S(2)}) async-start(bf16[32,32,2048]{2,1,0:T(8,128)(2,1)} %bitcast.62), calls=%async_computation.2 | async-start | bytes 8388608 | tf_op jit(solution)/shard_map/all_to_all | solution.py:94
  83.2 0.6 reduce-scatter.8.cloned.1.call-start
  83.8 8.4 %fusion.11 = f32[1024,768]{1,0:T(8,128)} fusion(bf16[1024,2048]{1,0:T(8,128)(2,1)} %bitcast.1, bf16[1,2048,768]{2,1,0:T(8,128)(2,1)} %param.15), kind=kOutput, calls=%fused_computation.27 | convolution fusion | flops 3221225472 | bytes 10485760 | tf_op jit(solution)/shard_map/dot_general | solution.py:14
  92.2 7.3 %fusion.7 = f32[1024,768]{1,0:T(8,128)} fusion(bf16[1024,2048]{1,0:T(8,128)(2,1)} %bitcast.1, bf16[1,2048,768]{2,1,0:T(8,128)(2,1)S(1)} %copy-done.3), kind=kOutput, calls=%fused_computation.23 | convolution fusion | flops 3221225472 | bytes 10485760 | tf_op jit(solution)/shard_map/dot_general | solution.py:15
  99.5 35.2 %all-to-all-done.2 = bf16[32,32,2048]{2,1,0:T(8,128)(2,1)} async-done(((bf16[32,32,2048]{2,1,0:T(8,128)(2,1)}), bf16[32,32,2048]{2,1,0:T(8,128)(2,1)}, u32[]{:S(2)}, u32[]{:S(2)}) %all-to-all-start.2) | async-done | bytes 4194336 | tf_op jit(solution)/shard_map/all_to_all | solution.py:94
  134.7 10.1 %multiply_convert_fusion.1 = (bf16[1024,768]{1,0:T(8,128)(2,1)}, bf16[1024,768]{1,0:T(8,128)(2,1)}, bf16[1024,768]{1,0:T(8,128)(2,1)S(1)}) fusion(f32[1024,768]{1,0:T(8,128)} %fusion.11, f32[1024,768]{1,0:T(8,128)} %fusion.7, bf16[1024,2048]{1,0:T(8,128)(2,1)} %bitcast.9, bf16[1,768,2048]{2,1,0:T(8,128)(2,1)S(1)} %copy-done), kind=kOutput, calls=%fused_computation.29 | convolution fusion | flops 3233808384 | bytes 18350080 | tf_op jit(solution)/shard_map/dot_general | solution.py:27
  144.8 1.1 copy-done.6
  146.0 7.0 %convolution_convert_fusion.2 = bf16[768,2048]{1,0:T(8,128)(2,1)} fusion(bf16[1024,768]{1,0:T(8,128)(2,1)S(1)} %get-tuple-element.22, bf16[1024,2048]{1,0:T(8,128)(2,1)} %bitcast.9), kind=kOutput, calls=%fused_computation.16 | convolution fusion | flops 3222798336 | bytes 8912896 | tf_op jit(solution)/shard_map/dot_general | solution.py:38
  153.0 0.2 reduce-scatter.6.cloned.1.call-start
  153.2 7.9 %convolution_convert_fusion.3 = bf16[2048,768]{1,0:T(8,128)(2,1)} fusion(bf16[1024,2048]{1,0:T(8,128)(2,1)} %bitcast.1, bf16[1024,768]{1,0:T(8,128)(2,1)} %get-tuple-element.20), kind=kOutput, calls=%fused_computation.17 | convolution fusion | flops 3222798336 | bytes 8912896 | tf_op jit(solution)/shard_map/dot_general | solution.py:37
  161.2 6.0 %fusion.9 = f32[1024,2048]{1,0:T(8,128)S(1)} fusion(bf16[1024,768]{1,0:T(8,128)(2,1)} %get-tuple-element.21, bf16[1,2048,768]{2,1,0:T(8,128)(2,1)} %param.15), kind=kOutput, calls=%fused_computation.25 | convolution fusion | flops 3221225472 | bytes 13107200 | tf_op jit(solution)/shard_map/dot_general | solution.py:33
  167.2 5.0 %add_convert_fusion = bf16[1024,2048]{1,0:T(8,128)(2,1)} fusion(f32[1024,2048]{1,0:T(8,128)S(1)} %fusion.9, bf16[1024,768]{1,0:T(8,128)(2,1)S(1)} %copy-done.7, bf16[1,2048,768]{2,1,0:T(8,128)(2,1)S(1)} %copy-done.4), kind=kOutput, calls=%fused_computation.7 | convolution fusion | flops 3225419776 | bytes 17301504 | tf_op jit(solution)/shard_map/dot_general | solution.py:34
  172.2 6.9 %all-to-all-start.3 = ((bf16[32,32,2048]{2,1,0:T(8,128)(2,1)}), bf16[32,32,2048]{2,1,0:T(8,128)(2,1)}, u32[]{:S(2)}, u32[]{:S(2)}) async-start(bf16[32,32,2048]{2,1,0:T(8,128)(2,1)} %bitcast.64), calls=%async_computation.3 | async-start | bytes 8388608 | tf_op jit(solution)/shard_map/all_to_all | solution.py:105
  179.1 0.3 reduce-scatter.4.cloned.1.call-start
  179.4 7.9 %convolution_convert_fusion.4 = bf16[2048,768]{1,0:T(8,128)(2,1)} fusion(bf16[1024,2048]{1,0:T(8,128)(2,1)} %bitcast.1, bf16[1024,768]{1,0:T(8,128)(2,1)} %get-tuple-element.21), kind=kOutput, calls=%fused_computation.18 | convolution fusion | flops 3222798336 | bytes 8912896 | tf_op jit(solution)/shard_map/dot_general | solution.py:36
  187.3 6.4 %convolution_convert_fusion = bf16[1024,2048]{1,0:T(8,128)(2,1)} fusion(bf16[1024,768]{1,0:T(8,128)(2,1)} %copy-done.6, bf16[1,768,2048]{2,1,0:T(8,128)(2,1)S(1)} %copy-done), kind=kOutput, calls=%fused_computation.14 | convolution fusion | flops 3223322624 | bytes 8912896 | tf_op jit(solution)/shard_map/dot_general | solution.py:18
  193.7 36.8 %all-to-all-done.3 = bf16[32,32,2048]{2,1,0:T(8,128)(2,1)} async-done(((bf16[32,32,2048]{2,1,0:T(8,128)(2,1)}), bf16[32,32,2048]{2,1,0:T(8,128)(2,1)}, u32[]{:S(2)}, u32[]{:S(2)}) %all-to-all-start.3) | async-done | bytes 4194336 | tf_op jit(solution)/shard_map/all_to_all | solution.py:105
  230.6 7.0 %all-to-all-start.1 = ((bf16[32,32,2048]{2,1,0:T(8,128)(2,1)}), bf16[32,32,2048]{2,1,0:T(8,128)(2,1)}, u32[]{:S(2)}, u32[]{:S(2)}) async-start(bf16[32,32,2048]{2,1,0:T(8,128)(2,1)} %bitcast.63), calls=%async_computation.1 | async-start | bytes 8388608 | tf_op jit(solution)/shard_map/all_to_all | solution.py:86
  237.6 0.1 copy.41
  237.8 2.1 convert_element_type.70
  240.0 0.1 copy.40
  240.2 0.1 copy.39
  240.3 0.6 fusion.15
  241.6 11.6 %gather_fusion.1 = bf16[1024,2048]{1,0:T(8,128)(2,1)} fusion(bf16[1024,2048]{1,0:T(8,128)(2,1)} %bitcast.11, s32[1024]{0:T(1024)S(1)} %broadcast_clamp_fusion), kind=kCustom, calls=%fused_computation.1.clone | custom fusion | bytes 8392704 | tf_op jit(solution)/shard_map/jit(_take)/gather | solution.py:118
  253.2 35.8 %all-to-all-done.1 = bf16[32,32,2048]{2,1,0:T(8,128)(2,1)} async-done(((bf16[32,32,2048]{2,1,0:T(8,128)(2,1)}), bf16[32,32,2048]{2,1,0:T(8,128)(2,1)}, u32[]{:S(2)}, u32[]{:S(2)}) %all-to-all-start.1) | async-done | bytes 4194336 | tf_op jit(solution)/shard_map/all_to_all | solution.py:86
  289.1 11.6 %gather_fusion = bf16[1024,2048]{1,0:T(8,128)(2,1)} fusion(bf16[1024,2048]{1,0:T(8,128)(2,1)} %bitcast.6, s32[1024]{0:T(1024)S(1)} %broadcast_clamp_fusion), kind=kCustom, calls=%fused_computation.clone | custom fusion | bytes 8392704 | tf_op jit(solution)/shard_map/jit(_take)/gather | solution.py:114
  300.6 0.7 collective-permute-start.2
  301.3 3.0 collective-permute-start.1
  304.4 11.5 %fusion.1 = (f32[128,8]{1,0:T(8,128)S(1)}, bf16[128,2048]{1,0:T(8,128)(2,1)}, bf16[128,2048]{1,0:T(8,128)(2,1)}) fusion(f32[128,2048]{1,0:T(8,128)} %convert_element_type.70, bf16[1024,2048]{1,0:T(8,128)(2,1)} %gather_fusion, pred[128,8]{1,0:T(8,128)(4,1)S(1)} %copy.39, f32[128,8]{1,0:T(8,128)S(1)} %copy.38, bf16[1024,2048]{1,0:T(8,128)(2,1)} %gather_fusion.1, ...), kind=kLoop, calls=%fused_computation.5 | loop fusion | flops 20446208 | bytes 10496000 | tf_op jit(solution)/shard_map/reduce_sum | solution.py:116
  315.9 0.8 collective-permute-start
  316.7 0.6 broadcast_select_fusion
  317.3 5.6 %collective-permute-done.2 = bf16[768,512]{1,0:T(8,128)(2,1)} collective-permute-done((bf16[768,512]{1,0:T(8,128)(2,1)}, bf16[768,512]{1,0:T(8,128)(2,1)}, u32[]{:S(2)}, u32[]{:S(2)}) %collective-permute-start.2) | collective-permute-done | bytes 786464 | tf_op jit(solution)/shard_map/ppermute | solution.py:10
  322.9 2.4 bitcast_convert_fusion
  325.3 14.5 %collective-permute-done.1 = bf16[512,768]{1,0:T(8,128)(2,1)} collective-permute-done((bf16[512,768]{1,0:T(8,128)(2,1)}, bf16[512,768]{1,0:T(8,128)(2,1)}, u32[]{:S(2)}, u32[]{:S(2)}) %collective-permute-start.1) | collective-permute-done | bytes 786464 | tf_op jit(solution)/shard_map/ppermute | solution.py:10
  339.8 1.3 bitcast_convert_fusion.1
  341.0 13.9 %collective-permute-done = bf16[512,768]{1,0:T(8,128)(2,1)S(1)} collective-permute-done((bf16[512,768]{1,0:T(8,128)(2,1)}, bf16[512,768]{1,0:T(8,128)(2,1)S(1)}, u32[]{:S(2)}, u32[]{:S(2)}) %collective-permute-start) | collective-permute-done | bytes 786464 | tf_op jit(solution)/shard_map/ppermute | solution.py:10
  355.0 1.2 bitcast_convert_fusion.2
  (26 shorter events, 0.3 us)
Async XLA Ops:
  7.2 127.5 %copy-start = (bf16[1,768,2048]{2,1,0:T(8,128)(2,1)S(1)}, bf16[1,768,2048]{2,1,0:T(8,128)(2,1)}, u32[]{:S(2)}) copy-start(bf16[1,768,2048]{2,1,0:T(8,128)(2,1)} %param.17) | copy-start | bytes 9437188
  16.5 59.9 %all-to-all-start = ((bf16[32,32,2048]{2,1,0:T(8,128)(2,1)}), bf16[32,32,2048]{2,1,0:T(8,128)(2,1)}, u32[]{:S(2)}, u32[]{:S(2)}) async-start(bf16[32,32,2048]{2,1,0:T(8,128)(2,1)} %bitcast.61), calls=%async_computation | async-start | bytes 8388608 | tf_op jit(solution)/shard_map/all_to_all | solution.py:75
  76.4 58.3 %all-to-all-start.2 = ((bf16[32,32,2048]{2,1,0:T(8,128)(2,1)}), bf16[32,32,2048]{2,1,0:T(8,128)(2,1)}, u32[]{:S(2)}, u32[]{:S(2)}) async-start(bf16[32,32,2048]{2,1,0:T(8,128)(2,1)} %bitcast.62), calls=%async_computation.2 | async-start | bytes 8388608 | tf_op jit(solution)/shard_map/all_to_all | solution.py:94
  83.2 217.4 %reduce-scatter.8.cloned.1.call-start = ((), (), s32[]{:S(2)}) async-start(), calls=%async_computation.9 | async-start | bytes 3932160 | tf_op jit(solution)/shard_map/reduce_scatter | solution.py:123
  83.8 8.4 %copy-start.3 = (bf16[1,2048,768]{2,1,0:T(8,128)(2,1)S(1)}, bf16[1,2048,768]{2,1,0:T(8,128)(2,1)}, u32[]{:S(2)}) copy-start(bf16[1,2048,768]{2,1,0:T(8,128)(2,1)} %param.16) | copy-start | bytes 9437188
  144.8 1.1 copy-start.6
  153.0 148.3 %reduce-scatter.6.cloned.1.call-start = ((), (), s32[]{:S(2)}) async-start(), calls=%async_computation.8 | async-start | bytes 3932160 | tf_op jit(solution)/shard_map/reduce_scatter | solution.py:123
  161.2 6.0 %copy-start.4 = (bf16[1,2048,768]{2,1,0:T(8,128)(2,1)S(1)}, bf16[1,2048,768]{2,1,0:T(8,128)(2,1)}, u32[]{:S(2)}) copy-start(bf16[1,2048,768]{2,1,0:T(8,128)(2,1)} %param.16) | copy-start | bytes 9437188
  161.2 6.0 %copy-start.7 = (bf16[1024,768]{1,0:T(8,128)(2,1)S(1)}, bf16[1024,768]{1,0:T(8,128)(2,1)}, u32[]{:S(2)}) copy-start(bf16[1024,768]{1,0:T(8,128)(2,1)} %get-tuple-element.20) | copy-start | bytes 4718596
  172.2 58.4 %all-to-all-start.3 = ((bf16[32,32,2048]{2,1,0:T(8,128)(2,1)}), bf16[32,32,2048]{2,1,0:T(8,128)(2,1)}, u32[]{:S(2)}, u32[]{:S(2)}) async-start(bf16[32,32,2048]{2,1,0:T(8,128)(2,1)} %bitcast.64), calls=%async_computation.3 | async-start | bytes 8388608 | tf_op jit(solution)/shard_map/all_to_all | solution.py:105
  179.1 136.8 %reduce-scatter.4.cloned.1.call-start = ((), (), s32[]{:S(2)}) async-start(), calls=%async_computation.7 | async-start | bytes 3932160 | tf_op jit(solution)/shard_map/reduce_scatter | solution.py:123
  230.6 9.7 %copy-start.5 = (s32[32]{0:T(128)S(1)}, s32[32]{0:T(128)}, u32[]{:S(2)}) copy-start(s32[32]{0:T(128)} %param.14) | copy-start | bytes 388
  230.6 58.5 %all-to-all-start.1 = ((bf16[32,32,2048]{2,1,0:T(8,128)(2,1)}), bf16[32,32,2048]{2,1,0:T(8,128)(2,1)}, u32[]{:S(2)}, u32[]{:S(2)}) async-start(bf16[32,32,2048]{2,1,0:T(8,128)(2,1)} %bitcast.63), calls=%async_computation.1 | async-start | bytes 8388608 | tf_op jit(solution)/shard_map/all_to_all | solution.py:86
  300.6 22.3 %collective-permute-start.2 = (bf16[768,512]{1,0:T(8,128)(2,1)}, bf16[768,512]{1,0:T(8,128)(2,1)}, u32[]{:S(2)}, u32[]{:S(2)}) collective-permute-start(bf16[768,512]{1,0:T(8,128)(2,1)} %reduce-scatter.8.cloned.1.call-done), channel_id=1, source_target_pairs={{0,64},{4,68},{8,72},{12,76},{16,80},{20,84},{24,88},{28,92},{32,9... | collective-permute-start | bytes 2359304 | tf_op jit(solution)/shard_map/ppermute | solution.py:10
  301.3 38.4 %collective-permute-start.1 = (bf16[512,768]{1,0:T(8,128)(2,1)}, bf16[512,768]{1,0:T(8,128)(2,1)}, u32[]{:S(2)}, u32[]{:S(2)}) collective-permute-start(bf16[512,768]{1,0:T(8,128)(2,1)} %reduce-scatter.6.cloned.1.call-done), channel_id=1, source_target_pairs={{0,64},{4,68},{8,72},{12,76},{16,80},{20,84},{24,88},{28,92},{32,9... | collective-permute-start | bytes 2359304 | tf_op jit(solution)/shard_map/ppermute | solution.py:10
  315.9 23.8 %copy-start.1 = (bf16[512,768]{1,0:T(8,128)(2,1)S(1)}, bf16[512,768]{1,0:T(8,128)(2,1)}, u32[]{:S(2)}) copy-start(bf16[512,768]{1,0:T(8,128)(2,1)} %reduce-scatter.6.cloned.1.call-done) | copy-start | bytes 2359300
  315.9 39.0 %collective-permute-start = (bf16[512,768]{1,0:T(8,128)(2,1)}, bf16[512,768]{1,0:T(8,128)(2,1)S(1)}, u32[]{:S(2)}, u32[]{:S(2)}) collective-permute-start(bf16[512,768]{1,0:T(8,128)(2,1)} %reduce-scatter.4.cloned.1.call-done), channel_id=1, source_target_pairs={{0,64},{4,68},{8,72},{12,76},{16,80},{20,84},{24,88},{28,92},{32,9... | collective-permute-start | bytes 2359304 | tf_op jit(solution)/shard_map/ppermute | solution.py:10
  317.3 37.7 %copy-start.2 = (bf16[512,768]{1,0:T(8,128)(2,1)S(1)}, bf16[512,768]{1,0:T(8,128)(2,1)}, u32[]{:S(2)}) copy-start(bf16[512,768]{1,0:T(8,128)(2,1)} %reduce-scatter.4.cloned.1.call-done) | copy-start | bytes 2359300
Sparse Core Ops, SparseCore 0:
  153.1 34.9 reduce-scatter.7
  190.5 37.9 reduce-scatter.5
  230.9 37.9 reduce-scatter.3

commit v2 on v1

v2 whole, which is shorter than its diff:
```python
import functools

import jax
import jax.numpy as jnp
from jax import lax
from jax.experimental import pallas as pl
from jax.experimental.pallas import tpu as pltpu
from jax.sharding import PartitionSpec as P

Z, X, C = 4, 4, 2
EXPERTS = Z * X * C
SLOTS = 32
TOK = 128
BLOCK = 512
VMEM = 58 << 20
TAGS = 128
BF16, F32 = jnp.bfloat16, jnp.float32
SHORT = pl.CostEstimate(flops=1 << 20, bytes_accessed=1 << 16, transcendentals=0)


def place(z, x, c):
    return (z % Z * X + x % X) * C + c


def moved(value, dz=0, dx=0, dc=0):
    pairs = [
        (place(z, x, c), place(z + dz, x + dx, c ^ dc))
        for z in range(Z)
        for x in range(X)
        for c in range(C)
    ]
    return lax.ppermute(value, "expert", pairs)


def along(value, axis, step):
    if step % 4 == 0:
        return value
    return moved(value, dz=step) if axis == "z" else moved(value, dx=step)


def slot_matrix(tags, experts):
    turned_tags = tags.astype(F32).T
    ids, weights = turned_tags[0:8], turned_tags[8:16] + turned_tags[16:24]
    named, weight = [], []
    for i in range(4):
        hit = ids == experts[i]
        named.append(jnp.max(jnp.where(hit, 1.0, 0.0), axis=0, keepdims=True))
        weight.append(jnp.sum(jnp.where(hit, weights, 0.0), axis=0, keepdims=True))
    named = jnp.concatenate(named + named, axis=0)
    weight = jnp.concatenate(weight, axis=0)
    before = lax.broadcasted_iota(jnp.int32, (TOK, TOK), 0) < lax.broadcasted_iota(
        jnp.int32, (TOK, TOK), 1
    )
    rank = jnp.dot(
        named.astype(BF16), before.astype(F32).astype(BF16), preferred_element_type=F32
    )
    key = jnp.where(named > 0, rank, -1.0)[:4]
    slots = lax.broadcasted_iota(jnp.int32, (4, SLOTS, TOK), 1).astype(F32)
    return jnp.where(key[:, None, :] == slots, 1.0, 0.0), weight


PART = 8 * SLOTS


def slots_at(source, expert, parts):
    at = source * SLOTS + (0 if parts > 1 else PART * expert)
    return pl.ds(at, SLOTS)


def source_specs(sources, block, column):
    return [pl.BlockSpec((TOK, block), lambda i, n, r=r: (r, column(i))) for _, r in sources]


def select_kernel(weighted, parts, numbers, *refs):
    tags, sources, outs, (matrix, scale) = refs[:8], refs[8:16], refs[16:-2], refs[-2:]

    @pl.when(pl.program_id(0) == 0)
    def _():
        experts = [numbers[i].astype(F32) for i in range(4)]
        for s in range(8):
            inside, weight = slot_matrix(tags[s][...], experts)
            matrix[s] = inside.reshape(TOK, TOK).astype(BF16)
            if weighted:
                scale[s] = jnp.sum(
                    (inside * weight[:, None, :]).reshape(TOK, TOK), axis=1, keepdims=True
                )

    for s in range(8):
        rows = jnp.dot(matrix[s], sources[s][...], preferred_element_type=F32)
        if weighted:
            rows = rows * scale[s]
        rows = rows.astype(BF16)
        for i in range(4):
            outs[i % parts][slots_at(s, i, parts), :] = rows[SLOTS * i : SLOTS * (i + 1), :]


def select(numbers, sources, weighted, parts):
    width = sources[0][0].shape[1] - TAGS
    height = 4 * PART // parts
    tags = source_specs(sources, TAGS, lambda i: width // TAGS)
    return pl.pallas_call(
        functools.partial(select_kernel, weighted, parts),
        grid_spec=pltpu.PrefetchScalarGridSpec(
            num_scalar_prefetch=1,
            grid=(width // BLOCK,),
            in_specs=tags + source_specs(sources, BLOCK, lambda i: i),
            out_specs=[pl.BlockSpec((height, BLOCK), lambda i, n: (0, i))] * parts,
            scratch_shapes=[
                pltpu.VMEM((8, TOK, TOK), BF16),
                pltpu.VMEM((8, TOK, 1), F32),
            ],
        ),
        out_shape=[jax.ShapeDtypeStruct((height, width), BF16)] * parts,
        compiler_params=pltpu.CompilerParams(vmem_limit_bytes=VMEM),
        cost_estimate=SHORT,
    )(numbers, *[v for v, _ in sources], *[v for v, _ in sources])


def combine_kernel(weighted, width, parts, numbers, *refs):
    tags, rows, (own, other, matrix) = refs[:8], refs[8:-3], refs[-3:]
    step = pl.program_id(0)

    @pl.when(step == 0)
    def _():
        experts = [numbers[i].astype(F32) for i in range(4)]
        for s in range(8):
            inside, weight = slot_matrix(tags[s][...], experts)
            if weighted:
                inside = inside * weight[:, None, :]
            matrix[s] = inside.reshape(TOK, TOK).T.astype(BF16)

    for s in range(8):
        held = jnp.concatenate(
            [rows[i % parts][slots_at(s, i, parts), :] for i in range(4)], axis=0
        )
        sums = jnp.dot(matrix[s], held, preferred_element_type=F32)
        at = pl.ds(pl.multiple_of(numbers[4 + s // 2] * TOK, TOK), TOK)
        if s % 2 == 0:
            own[at, :] = sums.astype(BF16)
        elif width % BLOCK == 0:
            other[at, :] = sums.astype(BF16)
        else:
            lanes = lax.broadcasted_iota(jnp.int32, sums.shape, 1)
            apart = jnp.where((lanes >= 8) & (lanes < 16), pltpu.roll(sums, 8, 1), 0.0)
            sums = jnp.where(step == width // BLOCK, apart, sums)
            other[at, :] = sums.astype(BF16)


def combine(numbers, sources, rows, weighted):
    width = rows[0].shape[1]
    parts = len(rows)
    tags_at = (sources[0][0].shape[1] - TAGS) // TAGS
    tags = source_specs(sources, TAGS, lambda i: tags_at)
    return pl.pallas_call(
        functools.partial(combine_kernel, weighted, width, parts),
        grid_spec=pltpu.PrefetchScalarGridSpec(
            num_scalar_prefetch=1,
            grid=(pl.cdiv(width, BLOCK),),
            in_specs=tags
            + [pl.BlockSpec((4 * PART // parts, BLOCK), lambda i, n: (0, i))] * parts,
            out_specs=[pl.BlockSpec((4 * TOK, BLOCK), lambda i, n: (0, i))] * 2,
            scratch_shapes=[pltpu.VMEM((8, TOK, TOK), BF16)],
        ),
        compiler_params=pltpu.CompilerParams(vmem_limit_bytes=VMEM),
        out_shape=[jax.ShapeDtypeStruct((4 * TOK, width), BF16)] * 2,
        cost_estimate=SHORT,
    )(numbers, *[v for v, _ in sources], *rows)


def forward_kernel(rows, gate_w, up_w, gate_pre, up_pre, activation):
    gate = dot(rows[...], gate_w[...], ((1,), (0,)))
    up = dot(rows[...], up_w[...], ((1,), (0,)))
    gate_pre[...] = gate
    up_pre[...] = up
    activation[...] = (gate * jax.nn.sigmoid(gate) * up).astype(BF16)


def forward(rows, gate_w, up_w):
    count, width = rows.shape
    hidden = gate_w.shape[1]
    weights = pl.BlockSpec((width, hidden), lambda i: (0, 0))
    block = pl.BlockSpec((PART, hidden), lambda i: (i, 0))
    shapes = [jax.ShapeDtypeStruct((count, hidden), t) for t in (F32, F32, BF16)]
    return pl.pallas_call(
        forward_kernel,
        grid=(count // PART,),
        in_specs=[pl.BlockSpec((PART, width), lambda i: (i, 0)), weights, weights],
        out_specs=[block] * 3,
        out_shape=shapes,
        compiler_params=pltpu.CompilerParams(vmem_limit_bytes=VMEM),
        cost_estimate=SHORT,
    )(rows, gate_w, up_w)


def out_kernel(activation, down_w, out):
    out[...] = dot(activation[...], down_w[...], ((1,), (0,))).astype(BF16)


def expert_output(activation, down_w):
    count, hidden = activation.shape
    width = down_w.shape[1]
    return pl.pallas_call(
        out_kernel,
        grid=(count // PART,),
        in_specs=[
            pl.BlockSpec((PART, hidden), lambda i: (i, 0)),
            pl.BlockSpec((hidden, width), lambda i: (0, 0)),
        ],
        out_specs=pl.BlockSpec((PART, width), lambda i: (i, 0)),
        out_shape=jax.ShapeDtypeStruct((count, width), BF16),
        compiler_params=pltpu.CompilerParams(vmem_limit_bytes=VMEM),
        cost_estimate=SHORT,
    )(activation, down_w)


def backward_kernel(g0, g1, g2, g3, down_w, gate_pre, up_pre, activation, *refs):
    gate_grad, up_grad, slots, down_part = refs
    grads, run = (g0, g1, g2, g3), C * SLOTS
    act = activation[...]
    down = None
    act_grads = []
    for j in range(4):
        act_grads.append(dot(grads[j][...], down_w[...], ((1,), (1,))))
        turned_act = jnp.concatenate(
            [act[(4 * k + j) * run : (4 * k + j + 1) * run] for k in range(4)], axis=0
        )
        term = dot(turned_act, grads[j][...], ((0,), (0,)))
        down = term if down is None else down + term
    down_part[...] = down.astype(BF16)
    for k in range(4):
        at = slice(k * PART, (k + 1) * PART)
        act_grad = jnp.concatenate(
            [act_grads[j][k * run : (k + 1) * run] for j in range(4)], axis=0
        )
        gate, up = gate_pre[at, :], up_pre[at, :]
        sigmoid = jax.nn.sigmoid(gate)
        gate_grad[at, :] = (act_grad * up * sigmoid * (1.0 + gate * (1.0 - sigmoid))).astype(BF16)
        up_grad[at, :] = (act_grad * gate * sigmoid).astype(BF16)
        term = jnp.sum(act[at].astype(F32) * act_grad, axis=1, keepdims=True)

        @pl.when(pl.program_id(0) == 0)
        def _(at=at, term=term):
            slots[at, :] = term

        @pl.when(pl.program_id(0) > 0)
        def _(at=at, term=term):
            slots[at, :] += term


def backward(grads, down_w, gate_pre, up_pre, activation):
    hidden, width = down_w.shape
    count, step = activation.shape[0], 256
    column = pl.BlockSpec((count, step), lambda i: (0, i))
    weights = pl.BlockSpec((step, width), lambda i: (i, 0))
    return pl.pallas_call(
        backward_kernel,
        grid=(hidden // step,),
        in_specs=[pl.BlockSpec((PART, width), lambda i: (0, 0))] * 4 + [weights] + [column] * 3,
        out_specs=[column, column, pl.BlockSpec((count, 1), lambda i: (0, 0)), weights],
        out_shape=[
            jax.ShapeDtypeStruct((count, hidden), BF16),
            jax.ShapeDtypeStruct((count, hidden), BF16),
            jax.ShapeDtypeStruct((count, 1), F32),
            jax.ShapeDtypeStruct((hidden, width), BF16),
        ],
        compiler_params=pltpu.CompilerParams(vmem_limit_bytes=VMEM),
        cost_estimate=SHORT,
    )(*grads, down_w, gate_pre, up_pre, activation)


def part_kernel(rows, grad, out):
    out[...] = dot(rows[...], grad[...], ((0,), (0,))).astype(BF16)


def weight_part(rows, grad):
    count, width = rows.shape
    hidden = grad.shape[1]
    return pl.pallas_call(
        part_kernel,
        grid=(width // BLOCK,),
        in_specs=[
            pl.BlockSpec((count, BLOCK), lambda i: (0, i)),
            pl.BlockSpec((count, hidden), lambda i: (0, 0)),
        ],
        out_specs=pl.BlockSpec((BLOCK, hidden), lambda i: (i, 0)),
        out_shape=jax.ShapeDtypeStruct((width, hidden), BF16),
        compiler_params=pltpu.CompilerParams(vmem_limit_bytes=VMEM),
        cost_estimate=SHORT,
    )(rows, grad)


def row_kernel(steps, gate_grad, up_grad, gate_w, up_w, high, low, *outs):
    step = pl.program_id(0)

    def put(rows):
        for k in range(4):
            for j in range(4):
                at = (k * 4 + j) * C * SLOTS
                outs[j][k * C * SLOTS : (k + 1) * C * SLOTS, :] = rows(j, at, at + C * SLOTS)

    @pl.when(step < steps)
    def _():
        wide = dot(gate_grad[...], gate_w[...], ((1,), (1,)))
        wide = (wide + dot(up_grad[...], up_w[...], ((1,), (1,)))).astype(BF16)
        put(lambda j, a, b: wide[a:b])

    @pl.when(step == steps)
    def _():
        lanes = lax.broadcasted_iota(jnp.int32, (C * SLOTS, BLOCK), 1)

        def rows(j, a, b):
            upper = jnp.where(lanes == j, high[a:b].astype(F32), 0.0)
            return jnp.where(lanes == 4 + j, low[a:b].astype(F32), upper).astype(BF16)

        put(rows)


def row_gradients(gate_grad, up_grad, gate_w, up_w, high, low):
    width, hidden = gate_w.shape
    steps = width // BLOCK
    whole = pl.BlockSpec(gate_grad.shape, lambda i: (0, 0))
    weights = pl.BlockSpec((BLOCK, hidden), lambda i: (jnp.minimum(i, steps - 1), 0))
    column = pl.BlockSpec(high.shape, lambda i: (0, 0))
    return pl.pallas_call(
        functools.partial(row_kernel, steps),
        grid=(steps + 1,),
        in_specs=[whole, whole, weights, weights, column, column],
        out_specs=[pl.BlockSpec((8 * SLOTS, BLOCK), lambda i: (0, i))] * 4,
        out_shape=[jax.ShapeDtypeStruct((8 * SLOTS, width + TAGS), BF16)] * 4,
        compiler_params=pltpu.CompilerParams(vmem_limit_bytes=VMEM),
        cost_estimate=SHORT,
    )(gate_grad, up_grad, gate_w, up_w, high, low)


def dot(a, b, contract):
    return lax.dot_general(a, b, (contract, ((), ())), preferred_element_type=F32)


def after(value, *earlier):
    return lax.optimization_barrier((value, earlier))[0]


def halves(value):
    high = value.astype(BF16)
    return high, (value - high.astype(F32)).astype(BF16)


def core_sum(parts):
    own, other = parts
    return (own.astype(F32) + moved(other, dc=1).astype(F32)).astype(BF16)


def after(value, *earlier):
    return lax.optimization_barrier((value, earlier))[0]


def halves(value):
    high = value.astype(BF16)
    return high, (value - high.astype(F32)).astype(BF16)


def core_sum(parts):
    own, other = parts
    return (own.astype(F32) + moved(other, dc=1).astype(F32)).astype(BF16)


def home(sums, axis):
    return [along(v, axis, -i).astype(F32) for i, v in enumerate(sums)]


def local(tokens, expert_ids, combine_weights, grad_output, swap_flags, w_gate, w_up, w_down):
    width = tokens.shape[1]
    me = lax.axis_index("expert")
    z, x, c = me // (X * C), me // C % X, me % C
    gate_w, up_w, down_w = w_gate[0], w_up[0], w_down[0]
    high, low = halves(combine_weights)
    tags = jnp.concatenate(
        [expert_ids.astype(BF16), high, low, jnp.zeros((TOK, TAGS - 24), BF16)], axis=1
    )

    along_x = [[place(i, j, k) for j in range(X)] for i in range(Z) for k in range(C)]
    along_z = [[place(i, j, k) for i in range(Z)] for j in range(X) for k in range(C)]

    def exchanged(v, groups=along_x):
        parts = v.reshape(4, -1, v.shape[1])
        parts = lax.all_to_all(parts, "expert", 0, 0, axis_index_groups=groups, tiled=True)
        return parts.reshape(v.shape)

    tagged = jnp.concatenate([tokens, tags], axis=1)
    legs = [along(tagged, "z", j) for j in range(4)]
    token_parts = [(v, 0) for part in legs for v in (part, moved(part, dc=1))]
    tagged = jnp.concatenate([grad_output, tags], axis=1)
    gathered = exchanged(jnp.concatenate([tagged] * X, axis=0))
    arrived = moved(gathered, dc=1)
    cotangent_parts = [(v, i) for i in range(X) for v in (gathered, arrived)]
    by_x = jnp.stack(
        [place(z, i, c) for i in range(X)] + [(z - j) % Z for j in range(4)]
    ).astype(jnp.int32)
    by_z = jnp.stack(
        [place(z + j, x, c) for j in range(4)] + [(x - i) % X for i in range(X)]
    ).astype(jnp.int32)

    rows = exchanged(select(by_x, token_parts, False, 1)[0])
    sent = select(by_z, cotangent_parts, True, 4)
    grads = [along(v, "z", j) for j, v in enumerate(sent)]

    gate_pre, up_pre, activation = forward(rows, gate_w, up_w)
    expert_out = expert_output(activation, down_w)
    back = exchanged(expert_out)
    gate_grad, up_grad, weight_slots, down_part = backward(
        grads, down_w, gate_pre, up_pre, after(activation, expert_out)
    )
    gate_part = weight_part(rows, gate_grad)
    gate_grad, up_grad, weight_slots = after((gate_grad, up_grad, weight_slots), gate_part)
    back_grads = row_gradients(gate_grad, up_grad, gate_w, up_w, *halves(weight_slots))
    back_grads = [along(v, "z", -j) for j, v in enumerate(back_grads)]
    numbers = jnp.arange(EXPERTS, dtype=jnp.int32)
    my_flag = jnp.sum(jnp.where(numbers == me, swap_flags, 0))

    def with_partners(mine):
        return mine, moved(mine, dz=Z // 2)

    def traded(pair):
        return jnp.where(my_flag == 1, pair[1], pair[0]).astype(F32)[None]

    down_pair = with_partners(lax.psum_scatter(down_part, "dp", scatter_dimension=1, tiled=True))
    up_part = weight_part(rows, after(up_grad, back, back_grads, down_pair))
    gate_pair = with_partners(lax.psum_scatter(gate_part, "dp", scatter_dimension=0, tiled=True))
    up_pair = with_partners(lax.psum_scatter(up_part, "dp", scatter_dimension=0, tiled=True))

    back = after(back, up_part, back_grads, down_pair)
    token_sums = core_sum(combine(by_x, token_parts, [back], True))
    cotangent_sums = core_sum(combine(after(by_z, token_sums), cotangent_parts, back_grads, False))
    arrived = exchanged(token_sums, along_z).reshape(Z, TOK, width)
    mixed = jnp.sum(arrived.astype(F32), axis=0).astype(BF16)
    cotangent_sums = after(cotangent_sums, token_sums)
    parts = [
        along(cotangent_sums[TOK * k : TOK * (k + 1)], "x", -k).astype(F32) for k in range(4)
    ]
    grad_tokens = sum(v[:, :width] for v in parts).astype(BF16)
    down_sum = traded(down_pair)
    gate_sum, up_sum = [traded(after(v, token_sums, cotangent_sums)) for v in (gate_pair, up_pair)]
    of_expert = jnp.concatenate([v[:, width : width + 16] for v in parts], axis=1)
    expert_at = jnp.stack(
        [place(z + j, x + k, c ^ b) for k in range(4) for b in range(C) for _ in range(2) for j in range(4)]
    )
    grad_weights = (
        jnp.sum(
            jnp.where(expert_ids[:, :, None] == expert_at, of_expert[:, None, :], 0.0), axis=2
        )
        / combine_weights
    )

    return (mixed, grad_tokens, grad_weights, gate_sum, up_sum, down_sum)


def solution(mesh):
    return jax.shard_map(
        local,
        mesh=mesh,
        in_specs=(
            P(("expert", "dp"), None),
            P(("expert", "dp"), None),
            P(("expert", "dp"), None),
            P(("expert", "dp"), None),
            P(),
            P("expert", None, None),
            P("expert", None, None),
            P("expert", None, None),
        ),
        out_specs=(
            P(("expert", "dp"), None),
            P(("expert", "dp"), None),
            P(("expert", "dp"), None),
            P("expert", "dp", None),
            P("expert", "dp", None),
            P("expert", None, "dp"),
        ),
        check_vma=False,
    )
```

time: 370 us -> 352 us (0.951); the launches traced: 363 us -> 349 us
  Pallas kernels: 0 us -> 87.3 us
  matrix products: 74.7 us -> 0 us
  local copies, waits for them, and re-layouts: 25 us -> 8.16 us
  waiting for transfers between devices: 187 us -> 172 us
  starting transfers between devices: 34.9 us -> 44.1 us
  other arithmetic: 26.6 us -> 22.5 us
    all_to_all x4, waiting for transfers between devices: 153 us -> 63 us  [exchanged(): lax.all_to_all(parts, 'expert', 0, 0, axis_index_groups=groups, tiled=True)]
    pallas_call x0 -> x10, Pallas kernels: none -> 87.3 us  [the longest x2 15 us: weight_part(): pl.pallas_call(part_kernel, grid=(width // BLOCK,), in_specs=[pl.BlockSpe...]
    dot_general x12 -> x0, matrix products: 74.7 us -> none  [the longest x1 10.1 us: expert_backward(): act_grad = jnp.dot(out_grad, down_w.T, preferred_element_type=jnp.float32)]
    ppermute x3 -> x22, waiting for transfers between devices: 34 us -> 103 us  [moved(): return lax.ppermute(value, 'expert', pairs)]
    gather x2 -> x0, local copies, waits for them, and re-layouts: 23.2 us -> none  [the longest x1 11.6 us: local(): jnp.take(returned_grads, safe_index, axis=0).astype(jnp.float32)]
    ppermute x3 -> x22, starting transfers between devices: 4.55 us -> 22.8 us  [moved(): return lax.ppermute(value, 'expert', pairs)]
    reduce_sum x4 -> x3, other arithmetic: 14.8 us -> 2.1 us  [the longest x1 1.31 us: local(): mixed = jnp.sum(arrived.astype(F32), axis=0).astype(BF16)]
    convert_element_type x1 -> x9, other arithmetic: 2.12 us -> 13.1 us  [the longest x2 6.57 us: core_sum(): return (own.astype(F32) + moved(other, dc=1).astype(F32)).astype(BF16)]
  transfers between devices with their start and end apart: 10 -> 29, of which waited for: 7 -> 10; matrix products, arithmetic and copies ran while one was open for 27% -> 6% of each run, Pallas kernels for 0% -> 21%
where the time goes in v2:
time: 352 us; the launch traced here: 349 us
  waiting for transfers between devices  172 us (49%)
  Pallas kernels  87.3 us (25%)
  starting transfers between devices  44.1 us (13%)
  other arithmetic  22.5 us (6%)
  between operations  14.6 us (4%)
  local copies, waits for them, and re-layouts  8.16 us (2%)
    ppermute x22, waiting for transfers between devices, moved(): return lax.ppermute(value, 'expert', pairs)  103 us
    all_to_all x4, waiting for transfers between devices, exchanged(): lax.all_to_all(parts, 'expert', 0, 0, axis_index_groups=groups, tiled=True)  63 us
    ppermute x22, starting transfers between devices, moved(): return lax.ppermute(value, 'expert', pairs)  22.8 us
    all_to_all x4, starting transfers between devices, exchanged(): lax.all_to_all(parts, 'expert', 0, 0, axis_index_groups=groups, tiled=True)  21.1 us
    pallas_call x2, Pallas kernels, weight_part(): pl.pallas_call(part_kernel, grid=(width // BLOCK,), in_specs=[pl.BlockSpe...  15 us
    pallas_call x1, Pallas kernels, backward(): pl.pallas_call(backward_kernel, grid=(hidden // step,), in_specs=[pl.Bloc...  14.7 us
    pallas_call x2, Pallas kernels, combine(): pl.pallas_call(functools.partial(combine_kernel, weighted, width, parts),...  14.3 us
    pallas_call x2, Pallas kernels, select(): pl.pallas_call(functools.partial(select_kernel, weighted, parts), grid_sp...  13.5 us
  transfers between devices with their start and end apart: 29, of which 10 were waited for; matrix products, arithmetic and copies ran while one was open for 6% of the time, Pallas kernels for 21%

profile of v2, /device:TPU:26, one launch (start us, length us, event | category | flops | bytes accessed | tf_op | source)
XLA Modules:
  0.0 348.9 jit_solution(16944651527101000343)
XLA Ops:
  8.2 0.8 copy.24
  9.0 1.2 concatenate.16
  10.2 1.5 pad_maximum_fusion
  11.7 5.0 %all-to-all-start.2 = ((bf16[4,128,2176]{2,1,0:T(8,128)(2,1)}), bf16[4,128,2176]{2,1,0:T(8,128)(2,1)S(1)}, u32[]{:S(2)}, u32[]{:S(2)}) async-start(bf16[4,128,2176]{2,1,0:T(8,128)(2,1)} %bitcast.84), calls=%async_computation.2 | async-start | bytes 4456448 | tf_op jit(solution)/shard_map/all_to_all | solution.py:386
  17.0 4.1 %collective-permute-start.5 = (bf16[128,2176]{1,0:T(8,128)(2,1)S(1)}, bf16[128,2176]{1,0:T(8,128)(2,1)S(1)}, u32[]{:S(2)}, u32[]{:S(2)}) collective-permute-start(bf16[128,2176]{1,0:T(8,128)(2,1)S(1)} %concatenate.15.refs_0_.refs_8_), channel_id=1, source_target_pairs={{0,96},{4,100},{8,104},{12,108},{16,112},{20,116},{24,120},{28,124... | collective-permute-start | bytes 1671176 | tf_op jit(solution)/shard_map/ppermute | solution.py:32
  21.1 1.3 collective-permute-start.1
  22.4 22.0 %collective-permute-done.5.refs_6_.refs_14_ = bf16[128,2176]{1,0:T(8,128)(2,1)S(1)} collective-permute-done((bf16[128,2176]{1,0:T(8,128)(2,1)S(1)}, bf16[128,2176]{1,0:T(8,128)(2,1)S(1)}, u32[]{:S(2)}, u32[]{:S(2)}) %collective-permute-start.5) | collective-permute-done | bytes 557088 | tf_op jit(solution)/shard_map/ppermute | solution.py:32
  44.9 3.0 collective-permute-done.1.refs_2_.refs_10_
  49.1 1.1 collective-permute-done.2.refs_3_.refs_11_
  50.2 6.7 %shard_map.127 = bf16[1024,2048]{1,0:T(8,128)(2,1)} custom-call(s32[8]{0:T(128)} %stack.185.numbers, bf16[128,2176]{1,0:T(8,128)(2,1)} %copy-done.1, bf16[128,2176]{1,0:T(8,128)(2,1)} %collective-permute-done.refs_1_.refs_9_, bf16[128,2176]{1,0:T(8,128)(2,1)} %collective-permute-done.1.refs_2_.refs_10_, ...), custom_call_target="tpu_custom_call" | custom-call | flops 1048576 | bytes 65536 | tf_op jit(solution)/shard_map/pallas_call | solution.py:101
  56.9 5.1 %all-to-all-start = ((bf16[4,256,2048]{2,1,0:T(8,128)(2,1)}), bf16[4,256,2048]{2,1,0:T(8,128)(2,1)}, u32[]{:S(2)}, u32[]{:S(2)}) async-start(bf16[4,256,2048]{2,1,0:T(8,128)(2,1)} %bitcast.76), calls=%async_computation | async-start | bytes 8388608 | tf_op jit(solution)/shard_map/all_to_all | solution.py:386
  62.6 6.8 %shard_map.130 = (bf16[256,2048]{1,0:T(8,128)(2,1)}, bf16[256,2048]{1,0:T(8,128)(2,1)}, bf16[256,2048]{1,0:T(8,128)(2,1)}, bf16[256,2048]{1,0:T(8,128)(2,1)}) custom-call(s32[8]{0:T(128)} %stack.194.numbers, bf16[512,2176]{1,0:T(8,128)(2,1)} %bitcast.64, ...), custom_call_target="tpu_custom_call" | custom-call | flops 1048576 | bytes 65536 | tf_op jit(solution)/shard_map/pallas_call | solution.py:101
  69.5 4.0 %collective-permute-start.9 = (bf16[256,2048]{1,0:T(8,128)(2,1)}, bf16[256,2048]{1,0:T(8,128)(2,1)S(1)}, u32[]{:S(2)}, u32[]{:S(2)}) collective-permute-start(bf16[256,2048]{1,0:T(8,128)(2,1)} %get-tuple-element.40), channel_id=1, source_target_pairs={{0,64},{4,68},{8,72},{12,76},{16,80},{20,84},{24,88},{28,92},{32,9... | collective-permute-start | bytes 3145736 | tf_op jit(solution)/shard_map/ppermute | solution.py:32
  73.5 36.5 %all-to-all-done = bf16[4,256,2048]{2,1,0:T(8,128)(2,1)} async-done(((bf16[4,256,2048]{2,1,0:T(8,128)(2,1)}), bf16[4,256,2048]{2,1,0:T(8,128)(2,1)}, u32[]{:S(2)}, u32[]{:S(2)}) %all-to-all-start) | async-done | bytes 4194336 | tf_op jit(solution)/shard_map/all_to_all | solution.py:386
  110.1 11.4 %shard_map.128 = (f32[1024,768]{1,0:T(8,128)}, f32[1024,768]{1,0:T(8,128)}, bf16[1024,768]{1,0:T(8,128)(2,1)}) custom-call(bf16[1024,2048]{1,0:T(8,128)(2,1)} %bitcast.9.rows, bf16[2048,768]{1,0:T(8,128)(2,1)} %bitcast.78, bf16[2048,768]{1,0:T(8,128)(2,1)} %bitcast.80), custom_call_target="tpu_custom_call" | custom-call | flops 1048576 | bytes 65536 | tf_op jit(solution)/shard_map/pallas_call | solution.py:184
  121.5 7.3 %shard_map.129 = bf16[1024,2048]{1,0:T(8,128)(2,1)} custom-call(bf16[1024,768]{1,0:T(8,128)(2,1)} %get-tuple-element.44.activation, bf16[768,2048]{1,0:T(8,128)(2,1)} %bitcast.82), custom_call_target="tpu_custom_call" | custom-call | flops 1048576 | bytes 65536 | tf_op jit(solution)/shard_map/pallas_call | solution.py:202
  128.9 1.0 copy-done.6
  130.6 14.7 %shard_map.131 = (bf16[1024,768]{1,0:T(8,128)(2,1)}, bf16[1024,768]{1,0:T(8,128)(2,1)}, f32[1024,1]{1,0:T(8,128)}, bf16[768,2048]{1,0:T(8,128)(2,1)}) custom-call(bf16[256,2048]{1,0:T(8,128)(2,1)} %get-tuple-element.38.g0, bf16[256,2048]{1,0:T(8,128)(2,1)} %copy-done.6, bf16[256,2048]{1,0:T(8,128)(2,1)} %copy-done.7, bf16[256,2048]{1,0:T(8,128)(2,1)} %copy-done.8, ...), custom_call_target="tpu_custom_call" | custom-call | flops 1048576 | bytes 65536 | tf_op jit(solution)/shard_map/pallas_call | solution.py:255
  145.6 7.4 %shard_map.132 = bf16[2048,768]{1,0:T(8,128)(2,1)} custom-call(bf16[1024,2048]{1,0:T(8,128)(2,1)} %bitcast.9.rows, bf16[1024,768]{1,0:T(8,128)(2,1)} %get-tuple-element.49.grad.gate_grad), custom_call_target="tpu_custom_call" | custom-call | flops 1048576 | bytes 65536 | tf_op jit(solution)/shard_map/pallas_call | solution.py:278
  153.0 6.4 %all-to-all-start.1 = ((bf16[4,256,2048]{2,1,0:T(8,128)(2,1)}), bf16[4,256,2048]{2,1,0:T(8,128)(2,1)}, u32[]{:S(2)}, u32[]{:S(2)}) async-start(bf16[4,256,2048]{2,1,0:T(8,128)(2,1)} %bitcast.77), calls=%async_computation.1 | async-start | bytes 8388608 | tf_op jit(solution)/shard_map/all_to_all | solution.py:386
  159.4 0.9 subtract_convert_fusion
  160.3 11.1 %shard_map.133 = (bf16[256,2176]{1,0:T(8,128)(2,1)}, bf16[256,2176]{1,0:T(8,128)(2,1)}, bf16[256,2176]{1,0:T(8,128)(2,1)}, bf16[256,2176]{1,0:T(8,128)(2,1)}) custom-call(bf16[1024,768]{1,0:T(8,128)(2,1)} %get-tuple-element.49.grad.gate_grad, bf16[1024,768]{1,0:T(8,128)(2,1)} %get-tuple-element.56.up_grad.grad, bf16[2048,768]{1,0:T(8,128)(2,1)} %bitcast.79, ...), custom_call_target="tpu_custom_call" | custom-call | flops 1048576 | bytes 65536 | tf_op jit(solution)/shard_map/pallas_call | solution.py:324
  171.3 2.7 collective-permute-start.11
  174.0 0.9 collective-permute-start.13
  175.0 6.6 %reduce-scatter.4.cloned.1.call-done = bf16[768,512]{1,0:T(8,128)(2,1)} async-done(((bf16[768,2048]{1,0:T(8,128)(2,1)}), bf16[768,512]{1,0:T(8,128)(2,1)}) %reduce-scatter.4.cloned.1.call-update) | async-done | bytes 786448 | tf_op jit(solution)/shard_map/reduce_scatter | solution.py:426
  181.6 3.1 collective-permute-start.14
  184.7 53.4 %collective-permute-done.11.refs_9_ = bf16[256,2176]{1,0:T(8,128)(2,1)S(1)} collective-permute-done((bf16[256,2176]{1,0:T(8,128)(2,1)}, bf16[256,2176]{1,0:T(8,128)(2,1)S(1)}, u32[]{:S(2)}, u32[]{:S(2)}) %collective-permute-start.11) | collective-permute-done | bytes 1114144 | tf_op jit(solution)/shard_map/ppermute | solution.py:32
  238.1 3.6 %collective-permute-done.14 = bf16[768,512]{1,0:T(8,128)(2,1)S(1)} collective-permute-done((bf16[768,512]{1,0:T(8,128)(2,1)}, bf16[768,512]{1,0:T(8,128)(2,1)S(1)}, u32[]{:S(2)}, u32[]{:S(2)}) %collective-permute-start.14) | collective-permute-done | bytes 786464 | tf_op jit(solution)/shard_map/ppermute | solution.py:32
  241.7 7.6 %shard_map.134 = bf16[2048,768]{1,0:T(8,128)(2,1)} custom-call(bf16[1024,2048]{1,0:T(8,128)(2,1)} %bitcast.9.rows, bf16[1024,768]{1,0:T(8,128)(2,1)} %get-tuple-element.56.up_grad.grad), custom_call_target="tpu_custom_call" | custom-call | flops 1048576 | bytes 65536 | tf_op jit(solution)/shard_map/pallas_call | solution.py:278
  249.3 6.6 %shard_map.135 = (bf16[512,2048]{1,0:T(8,128)(2,1)}, bf16[512,2048]{1,0:T(8,128)(2,1)}) custom-call(s32[8]{0:T(128)} %stack.185.numbers, bf16[128,2176]{1,0:T(8,128)(2,1)} %copy-done.1, bf16[128,2176]{1,0:T(8,128)(2,1)} %collective-permute-done.refs_1_.refs_9_, bf16[128,2176]{1,0:T(8,128)(2,1)} %collective-permute-done.1.refs_2_.refs_10_, ...), custom_call_target="tpu_custom_call" | custom-call | flops 1048576 | bytes 65536 | tf_op jit(solution)/shard_map/pallas_call | solution.py:154
  256.0 4.5 %collective-permute-done.15 = bf16[512,2048]{1,0:T(8,128)(2,1)} collective-permute-done((bf16[512,2048]{1,0:T(8,128)(2,1)}, bf16[512,2048]{1,0:T(8,128)(2,1)}, u32[]{:S(2)}, u32[]{:S(2)}) %collective-permute-start.15) | collective-permute-done | bytes 2097184 | tf_op jit(solution)/shard_map/ppermute | solution.py:32
  260.4 3.7 %add_convert_fusion.1 = bf16[512,2048]{1,0:T(8,128)(2,1)} fusion(bf16[512,2048]{1,0:T(8,128)(2,1)} %collective-permute-done.15, bf16[512,2048]{1,0:T(8,128)(2,1)S(1)} %copy-done.3), kind=kLoop, calls=%fused_computation.1 | loop fusion | flops 4194304 | bytes 6291456 | tf_op jit(solution)/shard_map/convert_element_type | solution.py:364
  264.2 7.8 %shard_map.136 = (bf16[512,2176]{1,0:T(8,128)(2,1)}, bf16[512,2176]{1,0:T(8,128)(2,1)}) custom-call(s32[8]{0:T(128)} %stack.194.numbers, bf16[512,2176]{1,0:T(8,128)(2,1)} %bitcast.72, bf16[512,2176]{1,0:T(8,128)(2,1)} %collective-permute-done.7.refs_1_.refs_3_.refs_5_.refs_7_.refs_9_.refs_11_.refs_13_.refs_15_, bf16[512,2176]{1,0:T(8,128)(2,1)} %bitcast.73, ...), custom_call_target="tpu_custom_call" | custom-call | flops 1048576 | bytes 65536 | tf_op jit(solution)/shard_map/pallas_call | solution.py:154
  272.4 4.6 %all-to-all-start.3 = ((bf16[4,128,2048]{2,1,0:T(8,128)(2,1)}), bf16[4,128,2048]{2,1,0:T(8,128)(2,1)S(1)}, u32[]{:S(2)}, u32[]{:S(2)}) async-start(bf16[4,128,2048]{2,1,0:T(8,128)(2,1)} %bitcast.25), calls=%async_computation.4 | async-start | bytes 4194304 | tf_op jit(solution)/shard_map/all_to_all | solution.py:386
  277.0 2.8 add_convert_fusion
  279.9 1.2 slice_convert_fusion
  281.1 1.5 collective-permute-start.19
  282.6 1.0 collective-permute-start.18
  283.5 2.3 collective-permute-start.17
  287.3 2.4 bitcast_convert_fusion
  289.7 26.5 %all-to-all-done.3 = bf16[4,128,2048]{2,1,0:T(8,128)(2,1)S(1)} async-done(((bf16[4,128,2048]{2,1,0:T(8,128)(2,1)}), bf16[4,128,2048]{2,1,0:T(8,128)(2,1)S(1)}, u32[]{:S(2)}, u32[]{:S(2)}) %all-to-all-start.3) | async-done | bytes 2097184 | tf_op jit(solution)/shard_map/all_to_all | solution.py:386
  316.2 1.3 reduce_sum.30
  321.0 1.1 convert_element_type.75
  322.2 1.1 convert_element_type.74
  323.3 1.1 convert_element_type.73
  324.5 1.1 fusion
  325.5 15.0 %collective-permute-done.21 = bf16[512,768]{1,0:T(8,128)(2,1)S(1)} collective-permute-done((bf16[512,768]{1,0:T(8,128)(2,1)}, bf16[512,768]{1,0:T(8,128)(2,1)S(1)}, u32[]{:S(2)}, u32[]{:S(2)}) %collective-permute-start.21) | collective-permute-done | bytes 786464 | tf_op jit(solution)/shard_map/ppermute | solution.py:32
  340.5 1.9 bitcast_convert_fusion.1
  (89 shorter events, 9.7 us)
Async XLA Ops:
  11.7 5.0 %copy-start.12 = (bf16[128,2048]{1,0:T(8,128)(2,1)S(1)}, bf16[128,2048]{1,0:T(8,128)(2,1)}, u32[]{:S(2)}) copy-start(bf16[128,2048]{1,0:T(8,128)(2,1)} %param.8) | copy-start | bytes 1572868
  11.7 36.1 %all-to-all-start.2 = ((bf16[4,128,2176]{2,1,0:T(8,128)(2,1)}), bf16[4,128,2176]{2,1,0:T(8,128)(2,1)S(1)}, u32[]{:S(2)}, u32[]{:S(2)}) async-start(bf16[4,128,2176]{2,1,0:T(8,128)(2,1)} %bitcast.84), calls=%async_computation.2 | async-start | bytes 4456448 | tf_op jit(solution)/shard_map/all_to_all | solution.py:386
  17.0 33.2 %copy-start.1 = (bf16[128,2176]{1,0:T(8,128)(2,1)}, bf16[128,2176]{1,0:T(8,128)(2,1)S(1)}, u32[]{:S(2)}) copy-start(bf16[128,2176]{1,0:T(8,128)(2,1)S(1)} %concatenate.15.refs_0_.refs_8_) | copy-start | bytes 1671172
  17.0 27.4 %collective-permute-start.5 = (bf16[128,2176]{1,0:T(8,128)(2,1)S(1)}, bf16[128,2176]{1,0:T(8,128)(2,1)S(1)}, u32[]{:S(2)}, u32[]{:S(2)}) collective-permute-start(bf16[128,2176]{1,0:T(8,128)(2,1)S(1)} %concatenate.15.refs_0_.refs_8_), channel_id=1, source_target_pairs={{0,96},{4,100},{8,104},{12,108},{16,112},{20,116},{24,120},{28,124... | collective-permute-start | bytes 1671176 | tf_op jit(solution)/shard_map/ppermute | solution.py:32
  21.1 23.3 %collective-permute-start.3 = (bf16[128,2176]{1,0:T(8,128)(2,1)S(1)}, bf16[128,2176]{1,0:T(8,128)(2,1)}, u32[]{:S(2)}, u32[]{:S(2)}) collective-permute-start(bf16[128,2176]{1,0:T(8,128)(2,1)S(1)} %concatenate.15.refs_0_.refs_8_), channel_id=1, source_target_pairs={{0,64},{4,68},{8,72},{12,76},{16,80},{20,84},{24,88},{28,92},{32,9... | collective-permute-start | bytes 1671176 | tf_op jit(solution)/shard_map/ppermute | solution.py:32
  21.1 26.8 %collective-permute-start.1 = (bf16[128,2176]{1,0:T(8,128)(2,1)S(1)}, bf16[128,2176]{1,0:T(8,128)(2,1)}, u32[]{:S(2)}, u32[]{:S(2)}) collective-permute-start(bf16[128,2176]{1,0:T(8,128)(2,1)S(1)} %concatenate.15.refs_0_.refs_8_), channel_id=1, source_target_pairs={{0,32},{4,36},{8,40},{12,44},{16,48},{20,52},{24,56},{28,60},{32,6... | collective-permute-start | bytes 1671176 | tf_op jit(solution)/shard_map/ppermute | solution.py:32
  22.4 26.7 %collective-permute-start = (bf16[128,2176]{1,0:T(8,128)(2,1)S(1)}, bf16[128,2176]{1,0:T(8,128)(2,1)}, u32[]{:S(2)}, u32[]{:S(2)}) collective-permute-start(bf16[128,2176]{1,0:T(8,128)(2,1)S(1)} %concatenate.15.refs_0_.refs_8_), channel_id=1, source_target_pairs={{0,4},{4,0},{8,12},{12,8},{16,20},{20,16},{24,28},{28,24},{32,36},... | collective-permute-start | bytes 1671176 | tf_op jit(solution)/shard_map/ppermute | solution.py:32
  44.4 5.8 %copy-start.2 = (bf16[128,2176]{1,0:T(8,128)(2,1)}, bf16[128,2176]{1,0:T(8,128)(2,1)S(1)}, u32[]{:S(2)}) copy-start(bf16[128,2176]{1,0:T(8,128)(2,1)S(1)} %collective-permute-done.5.refs_6_.refs_14_) | copy-start | bytes 1671172
  44.4 4.7 %collective-permute-start.6 = (bf16[128,2176]{1,0:T(8,128)(2,1)S(1)}, bf16[128,2176]{1,0:T(8,128)(2,1)}, u32[]{:S(2)}, u32[]{:S(2)}) collective-permute-start(bf16[128,2176]{1,0:T(8,128)(2,1)S(1)} %collective-permute-done.5.refs_6_.refs_14_), channel_id=1, source_target_pairs={{0,4},{4,0},{8,12},{12,8},{16,20},{20,16},{24,28},{28,24},{32,36},... | collective-permute-start | bytes 1671176 | tf_op jit(solution)/shard_map/ppermute | solution.py:32
  44.4 4.7 %collective-permute-start.4 = (bf16[128,2176]{1,0:T(8,128)(2,1)}, bf16[128,2176]{1,0:T(8,128)(2,1)}, u32[]{:S(2)}, u32[]{:S(2)}) collective-permute-start(bf16[128,2176]{1,0:T(8,128)(2,1)} %collective-permute-done.3.refs_4_.refs_12_), channel_id=1, source_target_pairs={{0,4},{4,0},{8,12},{12,8},{16,20},{20,16},{24,28},{28,24},{32,36},... | collective-permute-start | bytes 1671176 | tf_op jit(solution)/shard_map/ppermute | solution.py:32
  47.9 2.3 collective-permute-start.2
  47.9 9.0 %copy-start = (bf16[4,128,2176]{2,1,0:T(8,128)(2,1)}, bf16[4,128,2176]{2,1,0:T(8,128)(2,1)S(1)}, u32[]{:S(2)}) copy-start(bf16[4,128,2176]{2,1,0:T(8,128)(2,1)S(1)} %all-to-all-done.2) | copy-start | bytes 6684676
  47.9 14.8 %collective-permute-start.7 = (bf16[512,2176]{1,0:T(8,128)(2,1)S(1)}, bf16[512,2176]{1,0:T(8,128)(2,1)}, u32[]{:S(2)}, u32[]{:S(2)}) collective-permute-start(bf16[512,2176]{1,0:T(8,128)(2,1)S(1)} %bitcast.63), channel_id=1, source_target_pairs={{0,4},{4,0},{8,12},{12,8},{16,20},{20,16},{24,28},{28,24},{32,36},... | collective-permute-start | bytes 6684680 | tf_op jit(solution)/shard_map/ppermute | solution.py:32
  56.9 53.2 %all-to-all-start = ((bf16[4,256,2048]{2,1,0:T(8,128)(2,1)}), bf16[4,256,2048]{2,1,0:T(8,128)(2,1)}, u32[]{:S(2)}, u32[]{:S(2)}) async-start(bf16[4,256,2048]{2,1,0:T(8,128)(2,1)} %bitcast.76), calls=%async_computation | async-start | bytes 8388608 | tf_op jit(solution)/shard_map/all_to_all | solution.py:386
  62.0 119.6 %reduce-scatter.4.cloned.1.call-start = ((), (), s32[]{:S(2)}) async-start(), calls=%async_computation.7 | async-start | bytes 3932160 | tf_op jit(solution)/shard_map/reduce_scatter | solution.py:426
  69.4 59.4 %collective-permute-start.8 = (bf16[256,2048]{1,0:T(8,128)(2,1)}, bf16[256,2048]{1,0:T(8,128)(2,1)S(1)}, u32[]{:S(2)}, u32[]{:S(2)}) collective-permute-start(bf16[256,2048]{1,0:T(8,128)(2,1)} %get-tuple-element.39), channel_id=1, source_target_pairs={{0,32},{4,36},{8,40},{12,44},{16,48},{20,52},{24,56},{28,60},{32,6... | collective-permute-start | bytes 3145736 | tf_op jit(solution)/shard_map/ppermute | solution.py:32
  69.5 59.3 %collective-permute-start.9 = (bf16[256,2048]{1,0:T(8,128)(2,1)}, bf16[256,2048]{1,0:T(8,128)(2,1)S(1)}, u32[]{:S(2)}, u32[]{:S(2)}) collective-permute-start(bf16[256,2048]{1,0:T(8,128)(2,1)} %get-tuple-element.40), channel_id=1, source_target_pairs={{0,64},{4,68},{8,72},{12,76},{16,80},{20,84},{24,88},{28,92},{32,9... | collective-permute-start | bytes 3145736 | tf_op jit(solution)/shard_map/ppermute | solution.py:32
  73.5 55.3 %collective-permute-start.10 = (bf16[256,2048]{1,0:T(8,128)(2,1)}, bf16[256,2048]{1,0:T(8,128)(2,1)S(1)}, u32[]{:S(2)}, u32[]{:S(2)}) collective-permute-start(bf16[256,2048]{1,0:T(8,128)(2,1)} %get-tuple-element.41), channel_id=1, source_target_pairs={{0,96},{4,100},{8,104},{12,108},{16,112},{20,116},{24,120},{28,124... | collective-permute-start | bytes 3145736 | tf_op jit(solution)/shard_map/ppermute | solution.py:32
  128.8 1.0 copy-start.6
  128.8 1.5 copy-start.7
  128.9 1.8 copy-start.8
  145.4 126.8 %reduce-scatter.6.cloned.1.call-start = ((), (), s32[]{:S(2)}) async-start(), calls=%async_computation.8 | async-start | bytes 3932160 | tf_op jit(solution)/shard_map/reduce_scatter | solution.py:428
  153.0 6.4 %copy-start.13 = (f32[1024,1]{1,0:T(8,128)S(1)}, f32[1024,1]{1,0:T(8,128)}, u32[]{:S(2)}) copy-start(f32[1024,1]{1,0:T(8,128)} %get-tuple-element.50) | copy-start | bytes 12292
  153.0 85.1 %all-to-all-start.1 = ((bf16[4,256,2048]{2,1,0:T(8,128)(2,1)}), bf16[4,256,2048]{2,1,0:T(8,128)(2,1)}, u32[]{:S(2)}, u32[]{:S(2)}) async-start(bf16[4,256,2048]{2,1,0:T(8,128)(2,1)} %bitcast.77), calls=%async_computation.1 | async-start | bytes 8388608 | tf_op jit(solution)/shard_map/all_to_all | solution.py:386
  159.4 160.4 %reduce-scatter.8.cloned.1.call-start = ((), (), s32[]{:S(2)}) async-start(), calls=%async_computation.9 | async-start | bytes 3932160 | tf_op jit(solution)/shard_map/reduce_scatter | solution.py:429
  171.3 66.8 %collective-permute-start.11 = (bf16[256,2176]{1,0:T(8,128)(2,1)}, bf16[256,2176]{1,0:T(8,128)(2,1)S(1)}, u32[]{:S(2)}, u32[]{:S(2)}) collective-permute-start(bf16[256,2176]{1,0:T(8,128)(2,1)} %get-tuple-element.52), channel_id=1, source_target_pairs={{0,96},{4,100},{8,104},{12,108},{16,112},{20,116},{24,120},{28,124... | collective-permute-start | bytes 3342344 | tf_op jit(solution)/shard_map/ppermute | solution.py:32
  174.0 64.1 %collective-permute-start.12 = (bf16[256,2176]{1,0:T(8,128)(2,1)}, bf16[256,2176]{1,0:T(8,128)(2,1)S(1)}, u32[]{:S(2)}, u32[]{:S(2)}) collective-permute-start(bf16[256,2176]{1,0:T(8,128)(2,1)} %get-tuple-element.53), channel_id=1, source_target_pairs={{0,64},{4,68},{8,72},{12,76},{16,80},{20,84},{24,88},{28,92},{32,9... | collective-permute-start | bytes 3342344 | tf_op jit(solution)/shard_map/ppermute | solution.py:32
  174.0 64.1 %collective-permute-start.13 = (bf16[256,2176]{1,0:T(8,128)(2,1)}, bf16[256,2176]{1,0:T(8,128)(2,1)}, u32[]{:S(2)}, u32[]{:S(2)}) collective-permute-start(bf16[256,2176]{1,0:T(8,128)(2,1)} %get-tuple-element.54), channel_id=1, source_target_pairs={{0,32},{4,36},{8,40},{12,44},{16,48},{20,52},{24,56},{28,60},{32,6... | collective-permute-start | bytes 3342344 | tf_op jit(solution)/shard_map/ppermute | solution.py:32
  181.6 60.1 %collective-permute-start.14 = (bf16[768,512]{1,0:T(8,128)(2,1)}, bf16[768,512]{1,0:T(8,128)(2,1)S(1)}, u32[]{:S(2)}, u32[]{:S(2)}) collective-permute-start(bf16[768,512]{1,0:T(8,128)(2,1)} %reduce-scatter.4.cloned.1.call-done), channel_id=1, source_target_pairs={{0,64},{4,68},{8,72},{12,76},{16,80},{20,84},{24,88},{28,92},{32,9... | collective-permute-start | bytes 2359304 | tf_op jit(solution)/shard_map/ppermute | solution.py:32
  238.1 11.2 %copy-start.4 = (bf16[256,2176]{1,0:T(8,128)(2,1)}, bf16[256,2176]{1,0:T(8,128)(2,1)S(1)}, u32[]{:S(2)}) copy-start(bf16[256,2176]{1,0:T(8,128)(2,1)S(1)} %collective-permute-done.11.refs_9_) | copy-start | bytes 3342340
  238.1 11.2 %copy-start.5 = (bf16[256,2176]{1,0:T(8,128)(2,1)}, bf16[256,2176]{1,0:T(8,128)(2,1)S(1)}, u32[]{:S(2)}) copy-start(bf16[256,2176]{1,0:T(8,128)(2,1)S(1)} %collective-permute-done.12.refs_10_) | copy-start | bytes 3342340
  241.7 7.6 %copy-start.11 = (bf16[768,512]{1,0:T(8,128)(2,1)}, bf16[768,512]{1,0:T(8,128)(2,1)S(1)}, u32[]{:S(2)}) copy-start(bf16[768,512]{1,0:T(8,128)(2,1)S(1)} %collective-permute-done.14) | copy-start | bytes 2359300
  255.9 4.5 %copy-start.3 = (bf16[512,2048]{1,0:T(8,128)(2,1)S(1)}, bf16[512,2048]{1,0:T(8,128)(2,1)}, u32[]{:S(2)}) copy-start(bf16[512,2048]{1,0:T(8,128)(2,1)} %get-tuple-element.58) | copy-start | bytes 6291460
  255.9 4.5 %collective-permute-start.15 = (bf16[512,2048]{1,0:T(8,128)(2,1)}, bf16[512,2048]{1,0:T(8,128)(2,1)}, u32[]{:S(2)}, u32[]{:S(2)}) collective-permute-start(bf16[512,2048]{1,0:T(8,128)(2,1)} %get-tuple-element.59), channel_id=1, source_target_pairs={{0,4},{4,0},{8,12},{12,8},{16,20},{20,16},{24,28},{28,24},{32,36},... | collective-permute-start | bytes 6291464 | tf_op jit(solution)/shard_map/ppermute | solution.py:32
  271.9 5.1 %collective-permute-start.16 = (bf16[512,2176]{1,0:T(8,128)(2,1)}, bf16[512,2176]{1,0:T(8,128)(2,1)}, u32[]{:S(2)}, u32[]{:S(2)}) collective-permute-start(bf16[512,2176]{1,0:T(8,128)(2,1)} %get-tuple-element.62), channel_id=1, source_target_pairs={{0,4},{4,0},{8,12},{12,8},{16,20},{20,16},{24,28},{28,24},{32,36},... | collective-permute-start | bytes 6684680 | tf_op jit(solution)/shard_map/ppermute | solution.py:32
  272.2 45.3 %collective-permute-start.20 = (bf16[512,768]{1,0:T(8,128)(2,1)}, bf16[512,768]{1,0:T(8,128)(2,1)}, u32[]{:S(2)}, u32[]{:S(2)}) collective-permute-start(bf16[512,768]{1,0:T(8,128)(2,1)} %reduce-scatter.6.cloned.1.call-done), channel_id=1, source_target_pairs={{0,64},{4,68},{8,72},{12,76},{16,80},{20,84},{24,88},{28,92},{32,9... | collective-permute-start | bytes 2359304 | tf_op jit(solution)/shard_map/ppermute | solution.py:32
  272.4 43.7 %all-to-all-start.3 = ((bf16[4,128,2048]{2,1,0:T(8,128)(2,1)}), bf16[4,128,2048]{2,1,0:T(8,128)(2,1)S(1)}, u32[]{:S(2)}, u32[]{:S(2)}) async-start(bf16[4,128,2048]{2,1,0:T(8,128)(2,1)} %bitcast.25), calls=%async_computation.4 | async-start | bytes 4194304 | tf_op jit(solution)/shard_map/all_to_all | solution.py:386
  279.9 5.9 %copy-start.16 = (s32[32]{0:T(128)S(1)}, s32[32]{0:T(128)}, u32[]{:S(2)}) copy-start(s32[32]{0:T(128)} %param.12) | copy-start | bytes 388
  281.1 36.4 %collective-permute-start.19 = (bf16[128,2176]{1,0:T(8,128)(2,1)}, bf16[128,2176]{1,0:T(8,128)(2,1)}, u32[]{:S(2)}, u32[]{:S(2)}) collective-permute-start(bf16[128,2176]{1,0:T(8,128)(2,1)} %get-tuple-element.73), channel_id=1, source_target_pairs={{0,8},{4,12},{8,16},{12,20},{16,24},{20,28},{24,0},{28,4},{32,40},... | collective-permute-start | bytes 1671176 | tf_op jit(solution)/shard_map/ppermute | solution.py:32
  282.6 35.7 %collective-permute-start.18 = (bf16[128,2176]{1,0:T(8,128)(2,1)}, bf16[128,2176]{1,0:T(8,128)(2,1)}, u32[]{:S(2)}, u32[]{:S(2)}) collective-permute-start(bf16[128,2176]{1,0:T(8,128)(2,1)} %get-tuple-element.74), channel_id=1, source_target_pairs={{0,16},{4,20},{8,24},{12,28},{16,0},{20,4},{24,8},{28,12},{32,48},... | collective-permute-start | bytes 1671176 | tf_op jit(solution)/shard_map/ppermute | solution.py:32
  283.5 35.5 %collective-permute-start.17 = (bf16[128,2176]{1,0:T(8,128)(2,1)}, bf16[128,2176]{1,0:T(8,128)(2,1)}, u32[]{:S(2)}, u32[]{:S(2)}) collective-permute-start(bf16[128,2176]{1,0:T(8,128)(2,1)} %get-tuple-element.75), channel_id=1, source_target_pairs={{0,24},{4,28},{8,0},{12,4},{16,8},{20,12},{24,16},{28,20},{32,56},... | collective-permute-start | bytes 1671176 | tf_op jit(solution)/shard_map/ppermute | solution.py:32
  289.7 30.6 %copy-start.15 = (s32[128,8]{0,1:T(8,128)S(1)}, s32[128,8]{0,1:T(8,128)}, u32[]{:S(2)}) copy-start(s32[128,8]{0,1:T(8,128)} %param.9) | copy-start | bytes 12292
  289.7 30.7 %copy-start.14 = (f32[128,8]{0,1:T(8,128)S(1)}, f32[128,8]{0,1:T(8,128)}, u32[]{:S(2)}) copy-start(f32[128,8]{0,1:T(8,128)} %param.10) | copy-start | bytes 12292
  319.8 20.7 %collective-permute-start.21 = (bf16[512,768]{1,0:T(8,128)(2,1)}, bf16[512,768]{1,0:T(8,128)(2,1)S(1)}, u32[]{:S(2)}, u32[]{:S(2)}) collective-permute-start(bf16[512,768]{1,0:T(8,128)(2,1)} %reduce-scatter.8.cloned.1.call-done), channel_id=1, source_target_pairs={{0,64},{4,68},{8,72},{12,76},{16,80},{20,84},{24,88},{28,92},{32,9... | collective-permute-start | bytes 2359304 | tf_op jit(solution)/shard_map/ppermute | solution.py:32
  324.4 16.1 %copy-start.9 = (bf16[512,768]{1,0:T(8,128)(2,1)S(1)}, bf16[512,768]{1,0:T(8,128)(2,1)}, u32[]{:S(2)}) copy-start(bf16[512,768]{1,0:T(8,128)(2,1)} %reduce-scatter.6.cloned.1.call-done) | copy-start | bytes 2359300
  324.4 16.0 %copy-start.10 = (bf16[512,768]{1,0:T(8,128)(2,1)S(1)}, bf16[512,768]{1,0:T(8,128)(2,1)}, u32[]{:S(2)}) copy-start(bf16[512,768]{1,0:T(8,128)(2,1)} %reduce-scatter.8.cloned.1.call-done) | copy-start | bytes 2359300
Sparse Core Ops, SparseCore 0:
  145.5 36.0 reduce-scatter.3
  184.0 37.9 reduce-scatter.5
  256.1 35.2 reduce-scatter.7

commit v3 on v2

--- a/solution.py
+++ b/solution.py
@@ -424,12 +424,13 @@
         return jnp.where(my_flag == 1, pair[1], pair[0]).astype(F32)[None]
 
     down_pair = with_partners(lax.psum_scatter(down_part, "dp", scatter_dimension=1, tiled=True))
-    up_part = weight_part(rows, after(up_grad, back, back_grads, down_pair))
+    up_part = weight_part(rows, after(up_grad, back_grads))
     gate_pair = with_partners(lax.psum_scatter(gate_part, "dp", scatter_dimension=0, tiled=True))
     up_pair = with_partners(lax.psum_scatter(up_part, "dp", scatter_dimension=0, tiled=True))
 
-    back = after(back, up_part, back_grads, down_pair)
-    token_sums = core_sum(combine(by_x, token_parts, [back], True))
+    back = after(back, up_part, back_grads)
+    token_sums = combine(by_x, token_parts, [back], True)
+    token_sums = core_sum(after(token_sums, down_pair))
     cotangent_sums = core_sum(combine(after(by_z, token_sums), cotangent_parts, back_grads, False))
     arrived = exchanged(token_sums, along_z).reshape(Z, TOK, width)
     mixed = jnp.sum(arrived.astype(F32), axis=0).astype(BF16)

time: 352 us -> 352 us (level)
    all_to_all x4, waiting for transfers between devices: 63 us -> 80.2 us  [exchanged(): lax.all_to_all(parts, 'expert', 0, 0, axis_index_groups=groups, tiled=True)]
    ppermute x22, waiting for transfers between devices: 103 us -> 93.7 us  [moved(): return lax.ppermute(value, 'expert', pairs)]
    reduce_scatter x1, waiting for transfers between devices: 6.62 us -> 0.02 us  [local(): lax.psum_scatter(down_part, 'dp', scatter_dimension=1, tiled=True)]
  transfers between devices with their start and end apart: 29 -> 29, of which waited for: 10 -> 9; matrix products, arithmetic and copies ran while one was open for 6% -> 5% of each run, Pallas kernels for 21% -> 21%
where the time goes in v3:
time: 352 us; the launch traced here: 350 us
  waiting for transfers between devices  174 us (49%)
  Pallas kernels  87.5 us (25%)
  starting transfers between devices  43.6 us (12%)
  other arithmetic  22.7 us (6%)
  between operations  14.6 us (4%)
  local copies, waits for them, and re-layouts  8.03 us (2%)
    ppermute x22, waiting for transfers between devices, moved(): return lax.ppermute(value, 'expert', pairs)  93.7 us
    all_to_all x4, waiting for transfers between devices, exchanged(): lax.all_to_all(parts, 'expert', 0, 0, axis_index_groups=groups, tiled=True)  80.2 us
    ppermute x22, starting transfers between devices, moved(): return lax.ppermute(value, 'expert', pairs)  23.3 us
    all_to_all x4, starting transfers between devices, exchanged(): lax.all_to_all(parts, 'expert', 0, 0, axis_index_groups=groups, tiled=True)  20.1 us
    pallas_call x2, Pallas kernels, weight_part(): pl.pallas_call(part_kernel, grid=(width // BLOCK,), in_specs=[pl.BlockSpe...  15.1 us
    pallas_call x1, Pallas kernels, backward(): pl.pallas_call(backward_kernel, grid=(hidden // step,), in_specs=[pl.Bloc...  14.6 us
    pallas_call x2, Pallas kernels, combine(): pl.pallas_call(functools.partial(combine_kernel, weighted, width, parts),...  14.4 us
    pallas_call x2, Pallas kernels, select(): pl.pallas_call(functools.partial(select_kernel, weighted, parts), grid_sp...  13.5 us
  transfers between devices with their start and end apart: 29, of which 9 were waited for; matrix products, arithmetic and copies ran while one was open for 5% of the time, Pallas kernels for 21%

profile of v3, /device:TPU:26, one launch (start us, length us, event | category | flops | bytes accessed | tf_op | source)
XLA Modules:
  0.0 350.4 jit_solution(18039788896793213362)
XLA Ops:
  8.2 0.8 copy.24
  9.0 1.2 concatenate.16
  10.2 1.5 pad_maximum_fusion
  11.7 5.0 %all-to-all-start.2 = ((bf16[4,128,2176]{2,1,0:T(8,128)(2,1)}), bf16[4,128,2176]{2,1,0:T(8,128)(2,1)S(1)}, u32[]{:S(2)}, u32[]{:S(2)}) async-start(bf16[4,128,2176]{2,1,0:T(8,128)(2,1)} %bitcast.84), calls=%async_computation.2 | async-start | bytes 4456448 | tf_op jit(solution)/shard_map/all_to_all | solution.py:386
  17.0 4.1 %collective-permute-start.5 = (bf16[128,2176]{1,0:T(8,128)(2,1)S(1)}, bf16[128,2176]{1,0:T(8,128)(2,1)S(1)}, u32[]{:S(2)}, u32[]{:S(2)}) collective-permute-start(bf16[128,2176]{1,0:T(8,128)(2,1)S(1)} %concatenate.15.refs_0_.refs_8_), channel_id=1, source_target_pairs={{0,96},{4,100},{8,104},{12,108},{16,112},{20,116},{24,120},{28,124... | collective-permute-start | bytes 1671176 | tf_op jit(solution)/shard_map/ppermute | solution.py:32
  21.1 1.3 collective-permute-start.1
  22.4 22.0 %collective-permute-done.5.refs_6_.refs_14_ = bf16[128,2176]{1,0:T(8,128)(2,1)S(1)} collective-permute-done((bf16[128,2176]{1,0:T(8,128)(2,1)S(1)}, bf16[128,2176]{1,0:T(8,128)(2,1)S(1)}, u32[]{:S(2)}, u32[]{:S(2)}) %collective-permute-start.5) | collective-permute-done | bytes 557088 | tf_op jit(solution)/shard_map/ppermute | solution.py:32
  44.9 3.0 collective-permute-done.1.refs_2_.refs_10_
  49.1 1.1 collective-permute-done.2.refs_3_.refs_11_
  50.2 6.7 %shard_map.127 = bf16[1024,2048]{1,0:T(8,128)(2,1)} custom-call(s32[8]{0:T(128)} %stack.185.numbers, bf16[128,2176]{1,0:T(8,128)(2,1)} %copy-done.1, bf16[128,2176]{1,0:T(8,128)(2,1)} %collective-permute-done.refs_1_.refs_9_, bf16[128,2176]{1,0:T(8,128)(2,1)} %collective-permute-done.1.refs_2_.refs_10_, ...), custom_call_target="tpu_custom_call" | custom-call | flops 1048576 | bytes 65536 | tf_op jit(solution)/shard_map/pallas_call | solution.py:101
  56.9 5.1 %all-to-all-start = ((bf16[4,256,2048]{2,1,0:T(8,128)(2,1)}), bf16[4,256,2048]{2,1,0:T(8,128)(2,1)}, u32[]{:S(2)}, u32[]{:S(2)}) async-start(bf16[4,256,2048]{2,1,0:T(8,128)(2,1)} %bitcast.76), calls=%async_computation | async-start | bytes 8388608 | tf_op jit(solution)/shard_map/all_to_all | solution.py:386
  62.7 6.8 %shard_map.130 = (bf16[256,2048]{1,0:T(8,128)(2,1)}, bf16[256,2048]{1,0:T(8,128)(2,1)}, bf16[256,2048]{1,0:T(8,128)(2,1)}, bf16[256,2048]{1,0:T(8,128)(2,1)}) custom-call(s32[8]{0:T(128)} %stack.194.numbers, bf16[512,2176]{1,0:T(8,128)(2,1)} %bitcast.64, ...), custom_call_target="tpu_custom_call" | custom-call | flops 1048576 | bytes 65536 | tf_op jit(solution)/shard_map/pallas_call | solution.py:101
  69.5 4.0 %collective-permute-start.9 = (bf16[256,2048]{1,0:T(8,128)(2,1)}, bf16[256,2048]{1,0:T(8,128)(2,1)S(1)}, u32[]{:S(2)}, u32[]{:S(2)}) collective-permute-start(bf16[256,2048]{1,0:T(8,128)(2,1)} %get-tuple-element.42), channel_id=1, source_target_pairs={{0,64},{4,68},{8,72},{12,76},{16,80},{20,84},{24,88},{28,92},{32,9... | collective-permute-start | bytes 3145736 | tf_op jit(solution)/shard_map/ppermute | solution.py:32
  73.6 36.5 %all-to-all-done = bf16[4,256,2048]{2,1,0:T(8,128)(2,1)} async-done(((bf16[4,256,2048]{2,1,0:T(8,128)(2,1)}), bf16[4,256,2048]{2,1,0:T(8,128)(2,1)}, u32[]{:S(2)}, u32[]{:S(2)}) %all-to-all-start) | async-done | bytes 4194336 | tf_op jit(solution)/shard_map/all_to_all | solution.py:386
  110.1 11.4 %shard_map.128 = (f32[1024,768]{1,0:T(8,128)}, f32[1024,768]{1,0:T(8,128)}, bf16[1024,768]{1,0:T(8,128)(2,1)}) custom-call(bf16[1024,2048]{1,0:T(8,128)(2,1)} %bitcast.9.rows, bf16[2048,768]{1,0:T(8,128)(2,1)} %bitcast.78, bf16[2048,768]{1,0:T(8,128)(2,1)} %bitcast.80), custom_call_target="tpu_custom_call" | custom-call | flops 1048576 | bytes 65536 | tf_op jit(solution)/shard_map/pallas_call | solution.py:184
  121.5 7.3 %shard_map.129 = bf16[1024,2048]{1,0:T(8,128)(2,1)} custom-call(bf16[1024,768]{1,0:T(8,128)(2,1)} %get-tuple-element.46.activation, bf16[768,2048]{1,0:T(8,128)(2,1)} %bitcast.82), custom_call_target="tpu_custom_call" | custom-call | flops 1048576 | bytes 65536 | tf_op jit(solution)/shard_map/pallas_call | solution.py:202
  128.9 1.0 copy-done.6
  130.5 14.6 %shard_map.131 = (bf16[1024,768]{1,0:T(8,128)(2,1)}, bf16[1024,768]{1,0:T(8,128)(2,1)}, f32[1024,1]{1,0:T(8,128)}, bf16[768,2048]{1,0:T(8,128)(2,1)}) custom-call(bf16[256,2048]{1,0:T(8,128)(2,1)} %get-tuple-element.40.g0, bf16[256,2048]{1,0:T(8,128)(2,1)} %copy-done.6, bf16[256,2048]{1,0:T(8,128)(2,1)} %copy-done.7, bf16[256,2048]{1,0:T(8,128)(2,1)} %copy-done.8, ...), custom_call_target="tpu_custom_call" | custom-call | flops 1048576 | bytes 65536 | tf_op jit(solution)/shard_map/pallas_call | solution.py:255
  145.3 7.4 %shard_map.132 = bf16[2048,768]{1,0:T(8,128)(2,1)} custom-call(bf16[1024,2048]{1,0:T(8,128)(2,1)} %bitcast.9.rows, bf16[1024,768]{1,0:T(8,128)(2,1)} %get-tuple-element.51.grad.gate_grad), custom_call_target="tpu_custom_call" | custom-call | flops 1048576 | bytes 65536 | tf_op jit(solution)/shard_map/pallas_call | solution.py:278
  152.7 6.4 %all-to-all-start.1 = ((bf16[4,256,2048]{2,1,0:T(8,128)(2,1)}), bf16[4,256,2048]{2,1,0:T(8,128)(2,1)}, u32[]{:S(2)}, u32[]{:S(2)}) async-start(bf16[4,256,2048]{2,1,0:T(8,128)(2,1)} %bitcast.77), calls=%async_computation.1 | async-start | bytes 8388608 | tf_op jit(solution)/shard_map/all_to_all | solution.py:386
  159.1 0.9 subtract_convert_fusion
  160.0 11.1 %shard_map.133 = (bf16[256,2176]{1,0:T(8,128)(2,1)}, bf16[256,2176]{1,0:T(8,128)(2,1)}, bf16[256,2176]{1,0:T(8,128)(2,1)}, bf16[256,2176]{1,0:T(8,128)(2,1)}) custom-call(bf16[1024,768]{1,0:T(8,128)(2,1)} %get-tuple-element.51.grad.gate_grad, bf16[1024,768]{1,0:T(8,128)(2,1)} %get-tuple-element.57.up_grad.grad, bf16[2048,768]{1,0:T(8,128)(2,1)} %bitcast.79, ...), custom_call_target="tpu_custom_call" | custom-call | flops 1048576 | bytes 65536 | tf_op jit(solution)/shard_map/pallas_call | solution.py:324
  171.0 2.7 collective-permute-start.11
  173.7 0.9 collective-permute-start.13
  174.7 46.3 %collective-permute-done.11.refs_9_ = bf16[256,2176]{1,0:T(8,128)(2,1)S(1)} collective-permute-done((bf16[256,2176]{1,0:T(8,128)(2,1)}, bf16[256,2176]{1,0:T(8,128)(2,1)S(1)}, u32[]{:S(2)}, u32[]{:S(2)}) %collective-permute-start.11) | collective-permute-done | bytes 1114144 | tf_op jit(solution)/shard_map/ppermute | solution.py:32
  221.0 3.3 collective-permute-done.13.refs_11_
  224.2 7.8 %shard_map.134 = bf16[2048,768]{1,0:T(8,128)(2,1)} custom-call(bf16[1024,2048]{1,0:T(8,128)(2,1)} %bitcast.9.rows, bf16[1024,768]{1,0:T(8,128)(2,1)} %get-tuple-element.57.up_grad.grad), custom_call_target="tpu_custom_call" | custom-call | flops 1048576 | bytes 65536 | tf_op jit(solution)/shard_map/pallas_call | solution.py:278
  232.7 6.6 %shard_map.135 = (bf16[512,2048]{1,0:T(8,128)(2,1)}, bf16[512,2048]{1,0:T(8,128)(2,1)}) custom-call(s32[8]{0:T(128)} %stack.185.numbers, bf16[128,2176]{1,0:T(8,128)(2,1)} %copy-done.1, bf16[128,2176]{1,0:T(8,128)(2,1)} %collective-permute-done.refs_1_.refs_9_, bf16[128,2176]{1,0:T(8,128)(2,1)} %collective-permute-done.1.refs_2_.refs_10_, ...), custom_call_target="tpu_custom_call" | custom-call | flops 1048576 | bytes 65536 | tf_op jit(solution)/shard_map/pallas_call | solution.py:154
  239.3 13.7 %collective-permute-done.14 = bf16[768,512]{1,0:T(8,128)(2,1)S(1)} collective-permute-done((bf16[768,512]{1,0:T(8,128)(2,1)}, bf16[768,512]{1,0:T(8,128)(2,1)S(1)}, u32[]{:S(2)}, u32[]{:S(2)}) %collective-permute-start.14) | collective-permute-done | bytes 786464 | tf_op jit(solution)/shard_map/ppermute | solution.py:32
  253.0 4.4 %collective-permute-done.15 = bf16[512,2048]{1,0:T(8,128)(2,1)S(1)} collective-permute-done((bf16[512,2048]{1,0:T(8,128)(2,1)}, bf16[512,2048]{1,0:T(8,128)(2,1)S(1)}, u32[]{:S(2)}, u32[]{:S(2)}) %collective-permute-start.15) | collective-permute-done | bytes 2097184 | tf_op jit(solution)/shard_map/ppermute | solution.py:32
  257.3 3.8 %add_convert_fusion.1 = bf16[512,2048]{1,0:T(8,128)(2,1)} fusion(bf16[512,2048]{1,0:T(8,128)(2,1)S(1)} %collective-permute-done.15, bf16[512,2048]{1,0:T(8,128)(2,1)} %get-tuple-element.62), kind=kLoop, calls=%fused_computation.1 | loop fusion | flops 4194304 | bytes 6291456 | tf_op jit(solution)/shard_map/convert_element_type | solution.py:364
  261.1 7.9 %shard_map.136 = (bf16[512,2176]{1,0:T(8,128)(2,1)}, bf16[512,2176]{1,0:T(8,128)(2,1)}) custom-call(s32[8]{0:T(128)} %stack.194.numbers, bf16[512,2176]{1,0:T(8,128)(2,1)} %bitcast.72, bf16[512,2176]{1,0:T(8,128)(2,1)} %collective-permute-done.7.refs_1_.refs_3_.refs_5_.refs_7_.refs_9_.refs_11_.refs_13_.refs_15_, bf16[512,2176]{1,0:T(8,128)(2,1)} %bitcast.73, ...), custom_call_target="tpu_custom_call" | custom-call | flops 1048576 | bytes 65536 | tf_op jit(solution)/shard_map/pallas_call | solution.py:154
  270.6 1.0 collective-permute-start.20
  271.6 2.6 collective-permute-start.21
  274.2 3.6 %all-to-all-start.3 = ((bf16[4,128,2048]{2,1,0:T(8,128)(2,1)}), bf16[4,128,2048]{2,1,0:T(8,128)(2,1)S(1)}, u32[]{:S(2)}, u32[]{:S(2)}) async-start(bf16[4,128,2048]{2,1,0:T(8,128)(2,1)} %bitcast.25), calls=%async_computation.4 | async-start | bytes 4194304 | tf_op jit(solution)/shard_map/all_to_all | solution.py:386
  277.9 2.8 add_convert_fusion
  280.7 1.2 slice_convert_fusion
  281.9 1.5 collective-permute-start.19
  283.4 0.9 collective-permute-start.18
  284.3 2.3 collective-permute-start.17
  286.6 1.2 bitcast_convert_fusion
  287.9 43.7 %all-to-all-done.3 = bf16[4,128,2048]{2,1,0:T(8,128)(2,1)S(1)} async-done(((bf16[4,128,2048]{2,1,0:T(8,128)(2,1)}), bf16[4,128,2048]{2,1,0:T(8,128)(2,1)S(1)}, u32[]{:S(2)}, u32[]{:S(2)}) %all-to-all-start.3) | async-done | bytes 2097184 | tf_op jit(solution)/shard_map/all_to_all | solution.py:386
  331.6 1.3 reduce_sum.30
  332.9 3.3 bitcast_convert_fusion.1
  339.4 1.1 convert_element_type.75
  340.6 1.1 convert_element_type.74
  341.7 1.1 convert_element_type.73
  342.8 1.1 fusion
  (89 shorter events, 9.6 us)
Async XLA Ops:
  11.7 5.0 %copy-start.12 = (bf16[128,2048]{1,0:T(8,128)(2,1)S(1)}, bf16[128,2048]{1,0:T(8,128)(2,1)}, u32[]{:S(2)}) copy-start(bf16[128,2048]{1,0:T(8,128)(2,1)} %param.8) | copy-start | bytes 1572868
  11.7 36.1 %all-to-all-start.2 = ((bf16[4,128,2176]{2,1,0:T(8,128)(2,1)}), bf16[4,128,2176]{2,1,0:T(8,128)(2,1)S(1)}, u32[]{:S(2)}, u32[]{:S(2)}) async-start(bf16[4,128,2176]{2,1,0:T(8,128)(2,1)} %bitcast.84), calls=%async_computation.2 | async-start | bytes 4456448 | tf_op jit(solution)/shard_map/all_to_all | solution.py:386
  17.0 33.2 %copy-start.1 = (bf16[128,2176]{1,0:T(8,128)(2,1)}, bf16[128,2176]{1,0:T(8,128)(2,1)S(1)}, u32[]{:S(2)}) copy-start(bf16[128,2176]{1,0:T(8,128)(2,1)S(1)} %concatenate.15.refs_0_.refs_8_) | copy-start | bytes 1671172
  17.0 27.4 %collective-permute-start.5 = (bf16[128,2176]{1,0:T(8,128)(2,1)S(1)}, bf16[128,2176]{1,0:T(8,128)(2,1)S(1)}, u32[]{:S(2)}, u32[]{:S(2)}) collective-permute-start(bf16[128,2176]{1,0:T(8,128)(2,1)S(1)} %concatenate.15.refs_0_.refs_8_), channel_id=1, source_target_pairs={{0,96},{4,100},{8,104},{12,108},{16,112},{20,116},{24,120},{28,124... | collective-permute-start | bytes 1671176 | tf_op jit(solution)/shard_map/ppermute | solution.py:32
  21.1 23.3 %collective-permute-start.3 = (bf16[128,2176]{1,0:T(8,128)(2,1)S(1)}, bf16[128,2176]{1,0:T(8,128)(2,1)}, u32[]{:S(2)}, u32[]{:S(2)}) collective-permute-start(bf16[128,2176]{1,0:T(8,128)(2,1)S(1)} %concatenate.15.refs_0_.refs_8_), channel_id=1, source_target_pairs={{0,64},{4,68},{8,72},{12,76},{16,80},{20,84},{24,88},{28,92},{32,9... | collective-permute-start | bytes 1671176 | tf_op jit(solution)/shard_map/ppermute | solution.py:32
  21.1 26.8 %collective-permute-start.1 = (bf16[128,2176]{1,0:T(8,128)(2,1)S(1)}, bf16[128,2176]{1,0:T(8,128)(2,1)}, u32[]{:S(2)}, u32[]{:S(2)}) collective-permute-start(bf16[128,2176]{1,0:T(8,128)(2,1)S(1)} %concatenate.15.refs_0_.refs_8_), channel_id=1, source_target_pairs={{0,32},{4,36},{8,40},{12,44},{16,48},{20,52},{24,56},{28,60},{32,6... | collective-permute-start | bytes 1671176 | tf_op jit(solution)/shard_map/ppermute | solution.py:32
  22.4 26.7 %collective-permute-start = (bf16[128,2176]{1,0:T(8,128)(2,1)S(1)}, bf16[128,2176]{1,0:T(8,128)(2,1)}, u32[]{:S(2)}, u32[]{:S(2)}) collective-permute-start(bf16[128,2176]{1,0:T(8,128)(2,1)S(1)} %concatenate.15.refs_0_.refs_8_), channel_id=1, source_target_pairs={{0,4},{4,0},{8,12},{12,8},{16,20},{20,16},{24,28},{28,24},{32,36},... | collective-permute-start | bytes 1671176 | tf_op jit(solution)/shard_map/ppermute | solution.py:32
  44.4 5.8 %copy-start.2 = (bf16[128,2176]{1,0:T(8,128)(2,1)}, bf16[128,2176]{1,0:T(8,128)(2,1)S(1)}, u32[]{:S(2)}) copy-start(bf16[128,2176]{1,0:T(8,128)(2,1)S(1)} %collective-permute-done.5.refs_6_.refs_14_) | copy-start | bytes 1671172
  44.4 4.7 %collective-permute-start.6 = (bf16[128,2176]{1,0:T(8,128)(2,1)S(1)}, bf16[128,2176]{1,0:T(8,128)(2,1)}, u32[]{:S(2)}, u32[]{:S(2)}) collective-permute-start(bf16[128,2176]{1,0:T(8,128)(2,1)S(1)} %collective-permute-done.5.refs_6_.refs_14_), channel_id=1, source_target_pairs={{0,4},{4,0},{8,12},{12,8},{16,20},{20,16},{24,28},{28,24},{32,36},... | collective-permute-start | bytes 1671176 | tf_op jit(solution)/shard_map/ppermute | solution.py:32
  44.4 4.7 %collective-permute-start.4 = (bf16[128,2176]{1,0:T(8,128)(2,1)}, bf16[128,2176]{1,0:T(8,128)(2,1)}, u32[]{:S(2)}, u32[]{:S(2)}) collective-permute-start(bf16[128,2176]{1,0:T(8,128)(2,1)} %collective-permute-done.3.refs_4_.refs_12_), channel_id=1, source_target_pairs={{0,4},{4,0},{8,12},{12,8},{16,20},{20,16},{24,28},{28,24},{32,36},... | collective-permute-start | bytes 1671176 | tf_op jit(solution)/shard_map/ppermute | solution.py:32
  47.9 2.3 collective-permute-start.2
  47.9 9.0 %copy-start = (bf16[4,128,2176]{2,1,0:T(8,128)(2,1)}, bf16[4,128,2176]{2,1,0:T(8,128)(2,1)S(1)}, u32[]{:S(2)}) copy-start(bf16[4,128,2176]{2,1,0:T(8,128)(2,1)S(1)} %all-to-all-done.2) | copy-start | bytes 6684676
  47.9 14.8 %collective-permute-start.7 = (bf16[512,2176]{1,0:T(8,128)(2,1)S(1)}, bf16[512,2176]{1,0:T(8,128)(2,1)}, u32[]{:S(2)}, u32[]{:S(2)}) collective-permute-start(bf16[512,2176]{1,0:T(8,128)(2,1)S(1)} %bitcast.63), channel_id=1, source_target_pairs={{0,4},{4,0},{8,12},{12,8},{16,20},{20,16},{24,28},{28,24},{32,36},... | collective-permute-start | bytes 6684680 | tf_op jit(solution)/shard_map/ppermute | solution.py:32
  56.9 53.2 %all-to-all-start = ((bf16[4,256,2048]{2,1,0:T(8,128)(2,1)}), bf16[4,256,2048]{2,1,0:T(8,128)(2,1)}, u32[]{:S(2)}, u32[]{:S(2)}) async-start(bf16[4,256,2048]{2,1,0:T(8,128)(2,1)} %bitcast.76), calls=%async_computation | async-start | bytes 8388608 | tf_op jit(solution)/shard_map/all_to_all | solution.py:386
  62.0 170.0 %reduce-scatter.4.cloned.1.call-start = ((), (), s32[]{:S(2)}) async-start(), calls=%async_computation.7 | async-start | bytes 3932160 | tf_op jit(solution)/shard_map/reduce_scatter | solution.py:426
  69.5 59.4 %collective-permute-start.8 = (bf16[256,2048]{1,0:T(8,128)(2,1)}, bf16[256,2048]{1,0:T(8,128)(2,1)S(1)}, u32[]{:S(2)}, u32[]{:S(2)}) collective-permute-start(bf16[256,2048]{1,0:T(8,128)(2,1)} %get-tuple-element.41), channel_id=1, source_target_pairs={{0,32},{4,36},{8,40},{12,44},{16,48},{20,52},{24,56},{28,60},{32,6... | collective-permute-start | bytes 3145736 | tf_op jit(solution)/shard_map/ppermute | solution.py:32
  69.5 59.3 %collective-permute-start.9 = (bf16[256,2048]{1,0:T(8,128)(2,1)}, bf16[256,2048]{1,0:T(8,128)(2,1)S(1)}, u32[]{:S(2)}, u32[]{:S(2)}) collective-permute-start(bf16[256,2048]{1,0:T(8,128)(2,1)} %get-tuple-element.42), channel_id=1, source_target_pairs={{0,64},{4,68},{8,72},{12,76},{16,80},{20,84},{24,88},{28,92},{32,9... | collective-permute-start | bytes 3145736 | tf_op jit(solution)/shard_map/ppermute | solution.py:32
  73.6 55.3 %collective-permute-start.10 = (bf16[256,2048]{1,0:T(8,128)(2,1)}, bf16[256,2048]{1,0:T(8,128)(2,1)S(1)}, u32[]{:S(2)}, u32[]{:S(2)}) collective-permute-start(bf16[256,2048]{1,0:T(8,128)(2,1)} %get-tuple-element.43), channel_id=1, source_target_pairs={{0,96},{4,100},{8,104},{12,108},{16,112},{20,116},{24,120},{28,124... | collective-permute-start | bytes 3145736 | tf_op jit(solution)/shard_map/ppermute | solution.py:32
  128.8 1.0 copy-start.6
  128.8 1.3 copy-start.7
  128.9 1.6 copy-start.8
  145.1 125.5 %reduce-scatter.6.cloned.1.call-start = ((), (), s32[]{:S(2)}) async-start(), calls=%async_computation.8 | async-start | bytes 3932160 | tf_op jit(solution)/shard_map/reduce_scatter | solution.py:428
  152.7 6.4 %copy-start.13 = (f32[1024,1]{1,0:T(8,128)S(1)}, f32[1024,1]{1,0:T(8,128)}, u32[]{:S(2)}) copy-start(f32[1024,1]{1,0:T(8,128)} %get-tuple-element.52) | copy-start | bytes 12292
  152.7 80.0 %all-to-all-start.1 = ((bf16[4,256,2048]{2,1,0:T(8,128)(2,1)}), bf16[4,256,2048]{2,1,0:T(8,128)(2,1)}, u32[]{:S(2)}, u32[]{:S(2)}) async-start(bf16[4,256,2048]{2,1,0:T(8,128)(2,1)} %bitcast.77), calls=%async_computation.1 | async-start | bytes 8388608 | tf_op jit(solution)/shard_map/all_to_all | solution.py:386
  159.1 112.5 %reduce-scatter.8.cloned.1.call-start = ((), (), s32[]{:S(2)}) async-start(), calls=%async_computation.9 | async-start | bytes 3932160 | tf_op jit(solution)/shard_map/reduce_scatter | solution.py:429
  171.0 49.9 %collective-permute-start.11 = (bf16[256,2176]{1,0:T(8,128)(2,1)}, bf16[256,2176]{1,0:T(8,128)(2,1)S(1)}, u32[]{:S(2)}, u32[]{:S(2)}) collective-permute-start(bf16[256,2176]{1,0:T(8,128)(2,1)} %get-tuple-element.54), channel_id=1, source_target_pairs={{0,96},{4,100},{8,104},{12,108},{16,112},{20,116},{24,120},{28,124... | collective-permute-start | bytes 3342344 | tf_op jit(solution)/shard_map/ppermute | solution.py:32
  173.7 47.3 %collective-permute-start.12 = (bf16[256,2176]{1,0:T(8,128)(2,1)}, bf16[256,2176]{1,0:T(8,128)(2,1)S(1)}, u32[]{:S(2)}, u32[]{:S(2)}) collective-permute-start(bf16[256,2176]{1,0:T(8,128)(2,1)} %get-tuple-element.55), channel_id=1, source_target_pairs={{0,64},{4,68},{8,72},{12,76},{16,80},{20,84},{24,88},{28,92},{32,9... | collective-permute-start | bytes 3342344 | tf_op jit(solution)/shard_map/ppermute | solution.py:32
  173.7 50.5 %collective-permute-start.13 = (bf16[256,2176]{1,0:T(8,128)(2,1)}, bf16[256,2176]{1,0:T(8,128)(2,1)S(1)}, u32[]{:S(2)}, u32[]{:S(2)}) collective-permute-start(bf16[256,2176]{1,0:T(8,128)(2,1)} %get-tuple-element.56), channel_id=1, source_target_pairs={{0,32},{4,36},{8,40},{12,44},{16,48},{20,52},{24,56},{28,60},{32,6... | collective-permute-start | bytes 3342344 | tf_op jit(solution)/shard_map/ppermute | solution.py:32
  221.0 11.0 %copy-start.3 = (bf16[256,2176]{1,0:T(8,128)(2,1)}, bf16[256,2176]{1,0:T(8,128)(2,1)S(1)}, u32[]{:S(2)}) copy-start(bf16[256,2176]{1,0:T(8,128)(2,1)S(1)} %collective-permute-done.11.refs_9_) | copy-start | bytes 3342340
  221.0 11.0 %copy-start.4 = (bf16[256,2176]{1,0:T(8,128)(2,1)}, bf16[256,2176]{1,0:T(8,128)(2,1)S(1)}, u32[]{:S(2)}) copy-start(bf16[256,2176]{1,0:T(8,128)(2,1)S(1)} %collective-permute-done.12.refs_10_) | copy-start | bytes 3342340
  224.2 7.8 %copy-start.5 = (bf16[256,2176]{1,0:T(8,128)(2,1)}, bf16[256,2176]{1,0:T(8,128)(2,1)S(1)}, u32[]{:S(2)}) copy-start(bf16[256,2176]{1,0:T(8,128)(2,1)S(1)} %collective-permute-done.13.refs_11_) | copy-start | bytes 3342340
  232.1 20.9 %collective-permute-start.14 = (bf16[768,512]{1,0:T(8,128)(2,1)}, bf16[768,512]{1,0:T(8,128)(2,1)S(1)}, u32[]{:S(2)}, u32[]{:S(2)}) collective-permute-start(bf16[768,512]{1,0:T(8,128)(2,1)} %reduce-scatter.4.cloned.1.call-done), channel_id=1, source_target_pairs={{0,64},{4,68},{8,72},{12,76},{16,80},{20,84},{24,88},{28,92},{32,9... | collective-permute-start | bytes 2359304 | tf_op jit(solution)/shard_map/ppermute | solution.py:32
  253.0 8.1 %copy-start.10 = (bf16[768,512]{1,0:T(8,128)(2,1)}, bf16[768,512]{1,0:T(8,128)(2,1)S(1)}, u32[]{:S(2)}) copy-start(bf16[768,512]{1,0:T(8,128)(2,1)S(1)} %collective-permute-done.14) | copy-start | bytes 2359300
  253.0 4.4 %collective-permute-start.15 = (bf16[512,2048]{1,0:T(8,128)(2,1)}, bf16[512,2048]{1,0:T(8,128)(2,1)S(1)}, u32[]{:S(2)}, u32[]{:S(2)}) collective-permute-start(bf16[512,2048]{1,0:T(8,128)(2,1)} %get-tuple-element.63), channel_id=1, source_target_pairs={{0,4},{4,0},{8,12},{12,8},{16,20},{20,16},{24,28},{28,24},{32,36},... | collective-permute-start | bytes 6291464 | tf_op jit(solution)/shard_map/ppermute | solution.py:32
  261.1 8.1 %copy-start.16 = (s32[32]{0:T(128)S(1)}, s32[32]{0:T(128)}, u32[]{:S(2)}) copy-start(s32[32]{0:T(128)} %param.12) | copy-start | bytes 388
  269.0 8.9 %collective-permute-start.16 = (bf16[512,2176]{1,0:T(8,128)(2,1)}, bf16[512,2176]{1,0:T(8,128)(2,1)}, u32[]{:S(2)}, u32[]{:S(2)}) collective-permute-start(bf16[512,2176]{1,0:T(8,128)(2,1)} %get-tuple-element.66), channel_id=1, source_target_pairs={{0,4},{4,0},{8,12},{12,8},{16,20},{20,16},{24,28},{28,24},{32,36},... | collective-permute-start | bytes 6684680 | tf_op jit(solution)/shard_map/ppermute | solution.py:32
  270.6 62.3 %collective-permute-start.20 = (bf16[512,768]{1,0:T(8,128)(2,1)}, bf16[512,768]{1,0:T(8,128)(2,1)}, u32[]{:S(2)}, u32[]{:S(2)}) collective-permute-start(bf16[512,768]{1,0:T(8,128)(2,1)} %reduce-scatter.6.cloned.1.call-done), channel_id=1, source_target_pairs={{0,64},{4,68},{8,72},{12,76},{16,80},{20,84},{24,88},{28,92},{32,9... | collective-permute-start | bytes 2359304 | tf_op jit(solution)/shard_map/ppermute | solution.py:32
  271.6 61.3 %collective-permute-start.21 = (bf16[512,768]{1,0:T(8,128)(2,1)}, bf16[512,768]{1,0:T(8,128)(2,1)}, u32[]{:S(2)}, u32[]{:S(2)}) collective-permute-start(bf16[512,768]{1,0:T(8,128)(2,1)} %reduce-scatter.8.cloned.1.call-done), channel_id=1, source_target_pairs={{0,64},{4,68},{8,72},{12,76},{16,80},{20,84},{24,88},{28,92},{32,9... | collective-permute-start | bytes 2359304 | tf_op jit(solution)/shard_map/ppermute | solution.py:32
  274.2 57.3 %all-to-all-start.3 = ((bf16[4,128,2048]{2,1,0:T(8,128)(2,1)}), bf16[4,128,2048]{2,1,0:T(8,128)(2,1)S(1)}, u32[]{:S(2)}, u32[]{:S(2)}) async-start(bf16[4,128,2048]{2,1,0:T(8,128)(2,1)} %bitcast.25), calls=%async_computation.4 | async-start | bytes 4194304 | tf_op jit(solution)/shard_map/all_to_all | solution.py:386
  280.7 5.9 %copy-start.9 = (bf16[768,512]{1,0:T(8,128)(2,1)S(1)}, bf16[768,512]{1,0:T(8,128)(2,1)}, u32[]{:S(2)}) copy-start(bf16[768,512]{1,0:T(8,128)(2,1)} %reduce-scatter.4.cloned.1.call-done) | copy-start | bytes 2359300
  280.7 5.9 %copy-start.11 = (bf16[768,512]{1,0:T(8,128)(2,1)S(1)}, bf16[768,512]{1,0:T(8,128)(2,1)}, u32[]{:S(2)}) copy-start(bf16[768,512]{1,0:T(8,128)(2,1)} %copy-done.10) | copy-start | bytes 2359300
  281.9 54.3 %collective-permute-start.19 = (bf16[128,2176]{1,0:T(8,128)(2,1)}, bf16[128,2176]{1,0:T(8,128)(2,1)}, u32[]{:S(2)}, u32[]{:S(2)}) collective-permute-start(bf16[128,2176]{1,0:T(8,128)(2,1)} %get-tuple-element.77), channel_id=1, source_target_pairs={{0,8},{4,12},{8,16},{12,20},{16,24},{20,28},{24,0},{28,4},{32,40},... | collective-permute-start | bytes 1671176 | tf_op jit(solution)/shard_map/ppermute | solution.py:32
  283.4 53.6 %collective-permute-start.18 = (bf16[128,2176]{1,0:T(8,128)(2,1)}, bf16[128,2176]{1,0:T(8,128)(2,1)}, u32[]{:S(2)}, u32[]{:S(2)}) collective-permute-start(bf16[128,2176]{1,0:T(8,128)(2,1)} %get-tuple-element.78), channel_id=1, source_target_pairs={{0,16},{4,20},{8,24},{12,28},{16,0},{20,4},{24,8},{28,12},{32,48},... | collective-permute-start | bytes 1671176 | tf_op jit(solution)/shard_map/ppermute | solution.py:32
  284.3 53.4 %collective-permute-start.17 = (bf16[128,2176]{1,0:T(8,128)(2,1)}, bf16[128,2176]{1,0:T(8,128)(2,1)}, u32[]{:S(2)}, u32[]{:S(2)}) collective-permute-start(bf16[128,2176]{1,0:T(8,128)(2,1)} %get-tuple-element.79), channel_id=1, source_target_pairs={{0,24},{4,28},{8,0},{12,4},{16,8},{20,12},{24,16},{28,20},{32,56},... | collective-permute-start | bytes 1671176 | tf_op jit(solution)/shard_map/ppermute | solution.py:32
  332.9 5.8 %copy-start.15 = (s32[128,8]{0,1:T(8,128)S(1)}, s32[128,8]{0,1:T(8,128)}, u32[]{:S(2)}) copy-start(s32[128,8]{0,1:T(8,128)} %param.9) | copy-start | bytes 12292
  332.9 5.9 %copy-start.14 = (f32[128,8]{0,1:T(8,128)S(1)}, f32[128,8]{0,1:T(8,128)}, u32[]{:S(2)}) copy-start(f32[128,8]{0,1:T(8,128)} %param.10) | copy-start | bytes 12292
Sparse Core Ops, SparseCore 0:
  145.2 36.0 reduce-scatter.3
  183.7 37.9 reduce-scatter.5
  232.2 35.4 reduce-scatter.7

commit v4 on v3

--- a/solution.py
+++ b/solution.py
@@ -428,10 +428,9 @@
     gate_pair = with_partners(lax.psum_scatter(gate_part, "dp", scatter_dimension=0, tiled=True))
     up_pair = with_partners(lax.psum_scatter(up_part, "dp", scatter_dimension=0, tiled=True))
 
-    back = after(back, up_part, back_grads)
     token_sums = combine(by_x, token_parts, [back], True)
-    token_sums = core_sum(after(token_sums, down_pair))
-    cotangent_sums = core_sum(combine(after(by_z, token_sums), cotangent_parts, back_grads, False))
+    token_sums = core_sum(token_sums)
+    cotangent_sums = core_sum(combine(after(by_z, token_sums, up_part), cotangent_parts, back_grads, False))
     arrived = exchanged(token_sums, along_z).reshape(Z, TOK, width)
     mixed = jnp.sum(arrived.astype(F32), axis=0).astype(BF16)
     cotangent_sums = after(cotangent_sums, token_sums)

time: 352 us -> 346 us (0.983)
  waiting for transfers between devices: 174 us -> 165 us
    ppermute x22, waiting for transfers between devices: 93.7 us -> 80.9 us  [moved(): return lax.ppermute(value, 'expert', pairs)]
  transfers between devices with their start and end apart: 29 -> 29, of which waited for: 9 -> 11; matrix products, arithmetic and copies ran while one was open for 5% -> 7% of each run, Pallas kernels for 21% -> 19%
where the time goes in v4:
time: 346 us; the launch traced here: 344 us
  waiting for transfers between devices  165 us (48%)
  Pallas kernels  86.9 us (25%)
  starting transfers between devices  43.8 us (13%)
  other arithmetic  23.6 us (7%)
  between operations  14.6 us (4%)
  local copies, waits for them, and re-layouts  9.72 us (3%)
    all_to_all x4, waiting for transfers between devices, exchanged(): lax.all_to_all(parts, 'expert', 0, 0, axis_index_groups=groups, tiled=True)  83.6 us
    ppermute x22, waiting for transfers between devices, moved(): return lax.ppermute(value, 'expert', pairs)  80.9 us
    ppermute x22, starting transfers between devices, moved(): return lax.ppermute(value, 'expert', pairs)  23.6 us
    all_to_all x4, starting transfers between devices, exchanged(): lax.all_to_all(parts, 'expert', 0, 0, axis_index_groups=groups, tiled=True)  20.2 us
    pallas_call x2, Pallas kernels, weight_part(): pl.pallas_call(part_kernel, grid=(width // BLOCK,), in_specs=[pl.BlockSpe...  14.7 us
    pallas_call x1, Pallas kernels, backward(): pl.pallas_call(backward_kernel, grid=(hidden // step,), in_specs=[pl.Bloc...  14.6 us
    pallas_call x2, Pallas kernels, combine(): pl.pallas_call(functools.partial(combine_kernel, weighted, width, parts),...  14.5 us
    pallas_call x2, Pallas kernels, select(): pl.pallas_call(functools.partial(select_kernel, weighted, parts), grid_sp...  13.5 us
  transfers between devices with their start and end apart: 29, of which 11 were waited for; matrix products, arithmetic and copies ran while one was open for 7% of the time, Pallas kernels for 19%

profile of v4, /device:TPU:26, one launch (start us, length us, event | category | flops | bytes accessed | tf_op | source)
XLA Modules:
  0.0 344.0 jit_solution(7091279791372765392)
XLA Ops:
  9.0 1.2 concatenate.16
  10.2 1.6 pad_maximum_fusion
  11.8 5.0 %all-to-all-start.3 = ((bf16[4,128,2176]{2,1,0:T(8,128)(2,1)}), bf16[4,128,2176]{2,1,0:T(8,128)(2,1)S(1)}, u32[]{:S(2)}, u32[]{:S(2)}) async-start(bf16[4,128,2176]{2,1,0:T(8,128)(2,1)} %bitcast.84), calls=%async_computation.3 | async-start | bytes 4456448 | tf_op jit(solution)/shard_map/all_to_all | solution.py:386
  17.0 2.0 collective-permute-start.1
  19.0 3.6 %collective-permute-start.3 = (bf16[128,2176]{1,0:T(8,128)(2,1)S(1)}, bf16[128,2176]{1,0:T(8,128)(2,1)}, u32[]{:S(2)}, u32[]{:S(2)}) collective-permute-start(bf16[128,2176]{1,0:T(8,128)(2,1)S(1)} %concatenate.15.refs_0_.refs_8_), channel_id=1, source_target_pairs={{0,64},{4,68},{8,72},{12,76},{16,80},{20,84},{24,88},{28,92},{32,9... | collective-permute-start | bytes 1671176 | tf_op jit(solution)/shard_map/ppermute | solution.py:32
  22.6 1.0 collective-permute-start.5
  23.6 10.2 %collective-permute-done.1.refs_2_.refs_10_ = bf16[128,2176]{1,0:T(8,128)(2,1)S(1)} collective-permute-done((bf16[128,2176]{1,0:T(8,128)(2,1)S(1)}, bf16[128,2176]{1,0:T(8,128)(2,1)S(1)}, u32[]{:S(2)}, u32[]{:S(2)}) %collective-permute-start.1) | collective-permute-done | bytes 557088 | tf_op jit(solution)/shard_map/ppermute | solution.py:32
  33.8 12.6 %collective-permute-done.3.refs_4_.refs_12_ = bf16[128,2176]{1,0:T(8,128)(2,1)} collective-permute-done((bf16[128,2176]{1,0:T(8,128)(2,1)S(1)}, bf16[128,2176]{1,0:T(8,128)(2,1)}, u32[]{:S(2)}, u32[]{:S(2)}) %collective-permute-start.3) | collective-permute-done | bytes 557088 | tf_op jit(solution)/shard_map/ppermute | solution.py:32
  48.7 1.6 collective-permute-done.6.refs_7_.refs_15_
  50.3 6.7 %shard_map.127 = bf16[1024,2048]{1,0:T(8,128)(2,1)} custom-call(s32[8]{0:T(128)} %stack.185.numbers, bf16[128,2176]{1,0:T(8,128)(2,1)} %copy-done.1, bf16[128,2176]{1,0:T(8,128)(2,1)} %collective-permute-done.refs_1_.refs_9_, bf16[128,2176]{1,0:T(8,128)(2,1)} %copy-done.2, bf16[128,2176]{1,0:T(8,128)(2,1)} %collective-permute-done.2.refs_3_.refs_11_, ...), custom_call_target="tpu_custom_call" | custom-call | flops 1048576 | bytes 65536 | tf_op jit(solution)/shard_map/pallas_call | solution.py:101
  57.0 5.1 %all-to-all-start = ((bf16[4,256,2048]{2,1,0:T(8,128)(2,1)}), bf16[4,256,2048]{2,1,0:T(8,128)(2,1)}, u32[]{:S(2)}, u32[]{:S(2)}) async-start(bf16[4,256,2048]{2,1,0:T(8,128)(2,1)} %bitcast.76), calls=%async_computation | async-start | bytes 8388608 | tf_op jit(solution)/shard_map/all_to_all | solution.py:386
  62.8 6.8 %shard_map.131 = (bf16[256,2048]{1,0:T(8,128)(2,1)}, bf16[256,2048]{1,0:T(8,128)(2,1)}, bf16[256,2048]{1,0:T(8,128)(2,1)}, bf16[256,2048]{1,0:T(8,128)(2,1)}) custom-call(s32[8]{0:T(128)} %stack.194.numbers, bf16[512,2176]{1,0:T(8,128)(2,1)} %bitcast.64, ...), custom_call_target="tpu_custom_call" | custom-call | flops 1048576 | bytes 65536 | tf_op jit(solution)/shard_map/pallas_call | solution.py:101
  69.7 2.0 collective-permute-start.10
  71.7 1.2 collective-permute-start.11
  73.0 37.2 %all-to-all-done = bf16[4,256,2048]{2,1,0:T(8,128)(2,1)} async-done(((bf16[4,256,2048]{2,1,0:T(8,128)(2,1)}), bf16[4,256,2048]{2,1,0:T(8,128)(2,1)}, u32[]{:S(2)}, u32[]{:S(2)}) %all-to-all-start) | async-done | bytes 4194336 | tf_op jit(solution)/shard_map/all_to_all | solution.py:386
  110.2 11.4 %shard_map.128 = (f32[1024,768]{1,0:T(8,128)}, f32[1024,768]{1,0:T(8,128)}, bf16[1024,768]{1,0:T(8,128)(2,1)}) custom-call(bf16[1024,2048]{1,0:T(8,128)(2,1)} %bitcast.9.rows, bf16[2048,768]{1,0:T(8,128)(2,1)} %bitcast.78, bf16[2048,768]{1,0:T(8,128)(2,1)} %bitcast.80), custom_call_target="tpu_custom_call" | custom-call | flops 1048576 | bytes 65536 | tf_op jit(solution)/shard_map/pallas_call | solution.py:184
  121.6 7.3 %shard_map.129 = bf16[1024,2048]{1,0:T(8,128)(2,1)} custom-call(bf16[1024,768]{1,0:T(8,128)(2,1)} %get-tuple-element.45.activation, bf16[768,2048]{1,0:T(8,128)(2,1)} %bitcast.82), custom_call_target="tpu_custom_call" | custom-call | flops 1048576 | bytes 65536 | tf_op jit(solution)/shard_map/pallas_call | solution.py:202
  130.6 14.6 %shard_map.132 = (bf16[1024,768]{1,0:T(8,128)(2,1)}, bf16[1024,768]{1,0:T(8,128)(2,1)}, f32[1024,1]{1,0:T(8,128)}, bf16[768,2048]{1,0:T(8,128)(2,1)}) custom-call(bf16[256,2048]{1,0:T(8,128)(2,1)} %get-tuple-element.39.g0, bf16[256,2048]{1,0:T(8,128)(2,1)} %copy-done.6, bf16[256,2048]{1,0:T(8,128)(2,1)} %copy-done.7, bf16[256,2048]{1,0:T(8,128)(2,1)} %copy-done.8, ...), custom_call_target="tpu_custom_call" | custom-call | flops 1048576 | bytes 65536 | tf_op jit(solution)/shard_map/pallas_call | solution.py:255
  145.2 7.3 %shard_map.133 = bf16[2048,768]{1,0:T(8,128)(2,1)} custom-call(bf16[1024,2048]{1,0:T(8,128)(2,1)} %bitcast.9.rows, bf16[1024,768]{1,0:T(8,128)(2,1)} %get-tuple-element.50.grad.gate_grad), custom_call_target="tpu_custom_call" | custom-call | flops 1048576 | bytes 65536 | tf_op jit(solution)/shard_map/pallas_call | solution.py:278
  153.3 6.4 %all-to-all-start.1 = ((bf16[4,256,2048]{2,1,0:T(8,128)(2,1)}), bf16[4,256,2048]{2,1,0:T(8,128)(2,1)}, u32[]{:S(2)}, u32[]{:S(2)}) async-start(bf16[4,256,2048]{2,1,0:T(8,128)(2,1)} %bitcast.77), calls=%async_computation.1 | async-start | bytes 8388608 | tf_op jit(solution)/shard_map/all_to_all | solution.py:386
  160.6 11.0 %shard_map.134 = (bf16[256,2176]{1,0:T(8,128)(2,1)}, bf16[256,2176]{1,0:T(8,128)(2,1)}, bf16[256,2176]{1,0:T(8,128)(2,1)}, bf16[256,2176]{1,0:T(8,128)(2,1)}) custom-call(bf16[1024,768]{1,0:T(8,128)(2,1)} %get-tuple-element.50.grad.gate_grad, bf16[1024,768]{1,0:T(8,128)(2,1)} %get-tuple-element.56.up_grad.grad, bf16[2048,768]{1,0:T(8,128)(2,1)} %bitcast.79, ...), custom_call_target="tpu_custom_call" | custom-call | flops 1048576 | bytes 65536 | tf_op jit(solution)/shard_map/pallas_call | solution.py:324
  171.6 1.2 collective-permute-start.12
  172.8 1.0 collective-permute-start.13
  174.3 32.6 %all-to-all-done.1 = bf16[4,256,2048]{2,1,0:T(8,128)(2,1)} async-done(((bf16[4,256,2048]{2,1,0:T(8,128)(2,1)}), bf16[4,256,2048]{2,1,0:T(8,128)(2,1)}, u32[]{:S(2)}, u32[]{:S(2)}) %all-to-all-start.1) | async-done | bytes 4194336 | tf_op jit(solution)/shard_map/all_to_all | solution.py:386
  206.9 6.6 %shard_map.130 = (bf16[512,2048]{1,0:T(8,128)(2,1)}, bf16[512,2048]{1,0:T(8,128)(2,1)}) custom-call(s32[8]{0:T(128)} %stack.185.numbers, bf16[128,2176]{1,0:T(8,128)(2,1)} %copy-done.1, bf16[128,2176]{1,0:T(8,128)(2,1)} %collective-permute-done.refs_1_.refs_9_, bf16[128,2176]{1,0:T(8,128)(2,1)} %copy-done.2, ...), custom_call_target="tpu_custom_call" | custom-call | flops 1048576 | bytes 65536 | tf_op jit(solution)/shard_map/pallas_call | solution.py:154
  213.6 9.8 %collective-permute-done.14.refs_11_ = bf16[256,2176]{1,0:T(8,128)(2,1)} collective-permute-done((bf16[256,2176]{1,0:T(8,128)(2,1)}, bf16[256,2176]{1,0:T(8,128)(2,1)}, u32[]{:S(2)}, u32[]{:S(2)}) %collective-permute-start.14) | collective-permute-done | bytes 1114144 | tf_op jit(solution)/shard_map/ppermute | solution.py:32
  223.4 7.3 %shard_map.135 = bf16[2048,768]{1,0:T(8,128)(2,1)} custom-call(bf16[1024,2048]{1,0:T(8,128)(2,1)} %bitcast.9.rows, bf16[1024,768]{1,0:T(8,128)(2,1)} %get-tuple-element.56.up_grad.grad), custom_call_target="tpu_custom_call" | custom-call | flops 1048576 | bytes 65536 | tf_op jit(solution)/shard_map/pallas_call | solution.py:278
  230.8 1.6 copy-done.3
  232.3 3.7 %add_convert_fusion.1 = bf16[512,2048]{1,0:T(8,128)(2,1)} fusion(bf16[512,2048]{1,0:T(8,128)(2,1)} %collective-permute-done.7, bf16[512,2048]{1,0:T(8,128)(2,1)S(1)} %copy-done.3), kind=kLoop, calls=%fused_computation.1 | loop fusion | flops 4194304 | bytes 6291456 | tf_op jit(solution)/shard_map/convert_element_type | solution.py:364
  236.0 7.9 %shard_map.136 = (bf16[512,2176]{1,0:T(8,128)(2,1)}, bf16[512,2176]{1,0:T(8,128)(2,1)}) custom-call(s32[8]{0:T(128)} %stack.194.numbers, bf16[512,2176]{1,0:T(8,128)(2,1)} %bitcast.72, bf16[512,2176]{1,0:T(8,128)(2,1)} %collective-permute-done.8.refs_1_.refs_3_.refs_5_.refs_7_.refs_9_.refs_11_.refs_13_.refs_15_, bf16[512,2176]{1,0:T(8,128)(2,1)} %bitcast.73, ...), custom_call_target="tpu_custom_call" | custom-call | flops 1048576 | bytes 65536 | tf_op jit(solution)/shard_map/pallas_call | solution.py:154
  244.2 3.6 %all-to-all-start.2 = ((bf16[4,128,2048]{2,1,0:T(8,128)(2,1)}), bf16[4,128,2048]{2,1,0:T(8,128)(2,1)S(1)}, u32[]{:S(2)}, u32[]{:S(2)}) async-start(bf16[4,128,2048]{2,1,0:T(8,128)(2,1)} %bitcast.15), calls=%async_computation.2 | async-start | bytes 4194304 | tf_op jit(solution)/shard_map/all_to_all | solution.py:386
  247.9 3.5 %collective-permute-start.19 = (bf16[512,768]{1,0:T(8,128)(2,1)}, bf16[512,768]{1,0:T(8,128)(2,1)}, u32[]{:S(2)}, u32[]{:S(2)}) collective-permute-start(bf16[512,768]{1,0:T(8,128)(2,1)} %reduce-scatter.4.cloned.1.call-done), channel_id=1, source_target_pairs={{0,64},{4,68},{8,72},{12,76},{16,80},{20,84},{24,88},{28,92},{32,9... | collective-permute-start | bytes 2359304 | tf_op jit(solution)/shard_map/ppermute | solution.py:32
  251.5 2.8 add_convert_fusion
  254.3 1.2 slice_convert_fusion
  255.6 1.5 collective-permute-start.18
  257.6 2.6 collective-permute-start.16
  261.7 13.8 %all-to-all-done.2 = bf16[4,128,2048]{2,1,0:T(8,128)(2,1)S(1)} async-done(((bf16[4,128,2048]{2,1,0:T(8,128)(2,1)}), bf16[4,128,2048]{2,1,0:T(8,128)(2,1)S(1)}, u32[]{:S(2)}, u32[]{:S(2)}) %all-to-all-start.2) | async-done | bytes 2097184 | tf_op jit(solution)/shard_map/all_to_all | solution.py:386
  275.5 1.3 reduce_sum.30
  276.8 15.6 %collective-permute-done.19 = bf16[512,768]{1,0:T(8,128)(2,1)} collective-permute-done((bf16[512,768]{1,0:T(8,128)(2,1)}, bf16[512,768]{1,0:T(8,128)(2,1)}, u32[]{:S(2)}, u32[]{:S(2)}) %collective-permute-start.19) | collective-permute-done | bytes 786464 | tf_op jit(solution)/shard_map/ppermute | solution.py:32
  292.4 16.4 %collective-permute-done.21 = bf16[768,512]{1,0:T(8,128)(2,1)} collective-permute-done((bf16[768,512]{1,0:T(8,128)(2,1)}, bf16[768,512]{1,0:T(8,128)(2,1)}, u32[]{:S(2)}, u32[]{:S(2)}) %collective-permute-start.21) | collective-permute-done | bytes 786464 | tf_op jit(solution)/shard_map/ppermute | solution.py:32
  308.9 2.4 bitcast_convert_fusion
  313.6 1.8 collective-permute-start.20
  316.3 1.1 convert_element_type.75
  317.4 1.1 convert_element_type.74
  318.6 1.1 convert_element_type.73
  319.7 1.1 fusion
  320.8 13.6 %collective-permute-done.20 = bf16[512,768]{1,0:T(8,128)(2,1)S(1)} collective-permute-done((bf16[512,768]{1,0:T(8,128)(2,1)}, bf16[512,768]{1,0:T(8,128)(2,1)S(1)}, u32[]{:S(2)}, u32[]{:S(2)}) %collective-permute-start.20) | collective-permute-done | bytes 786464 | tf_op jit(solution)/shard_map/ppermute | solution.py:32
  334.4 3.0 bitcast_convert_fusion.1
  (87 shorter events, 14.1 us)
Async XLA Ops:
  11.8 5.0 %copy-start.11 = (bf16[128,2048]{1,0:T(8,128)(2,1)S(1)}, bf16[128,2048]{1,0:T(8,128)(2,1)}, u32[]{:S(2)}) copy-start(bf16[128,2048]{1,0:T(8,128)(2,1)} %param.8) | copy-start | bytes 1572868
  11.8 35.2 %all-to-all-start.3 = ((bf16[4,128,2176]{2,1,0:T(8,128)(2,1)}), bf16[4,128,2176]{2,1,0:T(8,128)(2,1)S(1)}, u32[]{:S(2)}, u32[]{:S(2)}) async-start(bf16[4,128,2176]{2,1,0:T(8,128)(2,1)} %bitcast.84), calls=%async_computation.3 | async-start | bytes 4456448 | tf_op jit(solution)/shard_map/all_to_all | solution.py:386
  17.0 33.3 %copy-start.1 = (bf16[128,2176]{1,0:T(8,128)(2,1)}, bf16[128,2176]{1,0:T(8,128)(2,1)S(1)}, u32[]{:S(2)}) copy-start(bf16[128,2176]{1,0:T(8,128)(2,1)S(1)} %concatenate.15.refs_0_.refs_8_) | copy-start | bytes 1671172
  17.0 16.8 %collective-permute-start.1 = (bf16[128,2176]{1,0:T(8,128)(2,1)S(1)}, bf16[128,2176]{1,0:T(8,128)(2,1)S(1)}, u32[]{:S(2)}, u32[]{:S(2)}) collective-permute-start(bf16[128,2176]{1,0:T(8,128)(2,1)S(1)} %concatenate.15.refs_0_.refs_8_), channel_id=1, source_target_pairs={{0,32},{4,36},{8,40},{12,44},{16,48},{20,52},{24,56},{28,60},{32,6... | collective-permute-start | bytes 1671176 | tf_op jit(solution)/shard_map/ppermute | solution.py:32
  19.0 27.4 %collective-permute-start.3 = (bf16[128,2176]{1,0:T(8,128)(2,1)S(1)}, bf16[128,2176]{1,0:T(8,128)(2,1)}, u32[]{:S(2)}, u32[]{:S(2)}) collective-permute-start(bf16[128,2176]{1,0:T(8,128)(2,1)S(1)} %concatenate.15.refs_0_.refs_8_), channel_id=1, source_target_pairs={{0,64},{4,68},{8,72},{12,76},{16,80},{20,84},{24,88},{28,92},{32,9... | collective-permute-start | bytes 1671176 | tf_op jit(solution)/shard_map/ppermute | solution.py:32
  22.6 23.8 %collective-permute-start.5 = (bf16[128,2176]{1,0:T(8,128)(2,1)S(1)}, bf16[128,2176]{1,0:T(8,128)(2,1)}, u32[]{:S(2)}, u32[]{:S(2)}) collective-permute-start(bf16[128,2176]{1,0:T(8,128)(2,1)S(1)} %concatenate.15.refs_0_.refs_8_), channel_id=1, source_target_pairs={{0,96},{4,100},{8,104},{12,108},{16,112},{20,116},{24,120},{28,124... | collective-permute-start | bytes 1671176 | tf_op jit(solution)/shard_map/ppermute | solution.py:32
  23.6 24.2 %collective-permute-start = (bf16[128,2176]{1,0:T(8,128)(2,1)S(1)}, bf16[128,2176]{1,0:T(8,128)(2,1)}, u32[]{:S(2)}, u32[]{:S(2)}) collective-permute-start(bf16[128,2176]{1,0:T(8,128)(2,1)S(1)} %concatenate.15.refs_0_.refs_8_), channel_id=1, source_target_pairs={{0,4},{4,0},{8,12},{12,8},{16,20},{20,16},{24,28},{28,24},{32,36},... | collective-permute-start | bytes 1671176 | tf_op jit(solution)/shard_map/ppermute | solution.py:32
  33.8 16.5 %copy-start.2 = (bf16[128,2176]{1,0:T(8,128)(2,1)}, bf16[128,2176]{1,0:T(8,128)(2,1)S(1)}, u32[]{:S(2)}) copy-start(bf16[128,2176]{1,0:T(8,128)(2,1)S(1)} %collective-permute-done.1.refs_2_.refs_10_) | copy-start | bytes 1671172
  33.8 14.0 %collective-permute-start.2 = (bf16[128,2176]{1,0:T(8,128)(2,1)S(1)}, bf16[128,2176]{1,0:T(8,128)(2,1)}, u32[]{:S(2)}, u32[]{:S(2)}) collective-permute-start(bf16[128,2176]{1,0:T(8,128)(2,1)S(1)} %collective-permute-done.1.refs_2_.refs_10_), channel_id=1, source_target_pairs={{0,4},{4,0},{8,12},{12,8},{16,20},{20,16},{24,28},{28,24},{32,36},... | collective-permute-start | bytes 1671176 | tf_op jit(solution)/shard_map/ppermute | solution.py:32
  46.4 2.3 collective-permute-start.4
  46.4 3.9 %collective-permute-start.6 = (bf16[128,2176]{1,0:T(8,128)(2,1)}, bf16[128,2176]{1,0:T(8,128)(2,1)}, u32[]{:S(2)}, u32[]{:S(2)}) collective-permute-start(bf16[128,2176]{1,0:T(8,128)(2,1)} %collective-permute-done.5.refs_6_.refs_14_), channel_id=1, source_target_pairs={{0,4},{4,0},{8,12},{12,8},{16,20},{20,16},{24,28},{28,24},{32,36},... | collective-permute-start | bytes 1671176 | tf_op jit(solution)/shard_map/ppermute | solution.py:32
  46.9 10.1 %copy-start = (bf16[4,128,2176]{2,1,0:T(8,128)(2,1)}, bf16[4,128,2176]{2,1,0:T(8,128)(2,1)S(1)}, u32[]{:S(2)}) copy-start(bf16[4,128,2176]{2,1,0:T(8,128)(2,1)S(1)} %all-to-all-done.3) | copy-start | bytes 6684676
  46.9 15.9 %collective-permute-start.8 = (bf16[512,2176]{1,0:T(8,128)(2,1)S(1)}, bf16[512,2176]{1,0:T(8,128)(2,1)}, u32[]{:S(2)}, u32[]{:S(2)}) collective-permute-start(bf16[512,2176]{1,0:T(8,128)(2,1)S(1)} %bitcast.63), channel_id=1, source_target_pairs={{0,4},{4,0},{8,12},{12,8},{16,20},{20,16},{24,28},{28,24},{32,36},... | collective-permute-start | bytes 6684680 | tf_op jit(solution)/shard_map/ppermute | solution.py:32
  57.0 53.2 %all-to-all-start = ((bf16[4,256,2048]{2,1,0:T(8,128)(2,1)}), bf16[4,256,2048]{2,1,0:T(8,128)(2,1)}, u32[]{:S(2)}, u32[]{:S(2)}) async-start(bf16[4,256,2048]{2,1,0:T(8,128)(2,1)} %bitcast.76), calls=%async_computation | async-start | bytes 8388608 | tf_op jit(solution)/shard_map/all_to_all | solution.py:386
  62.1 185.7 %reduce-scatter.4.cloned.1.call-start = ((), (), s32[]{:S(2)}) async-start(), calls=%async_computation.7 | async-start | bytes 3932160 | tf_op jit(solution)/shard_map/reduce_scatter | solution.py:428
  69.6 59.3 %collective-permute-start.9 = (bf16[256,2048]{1,0:T(8,128)(2,1)}, bf16[256,2048]{1,0:T(8,128)(2,1)S(1)}, u32[]{:S(2)}, u32[]{:S(2)}) collective-permute-start(bf16[256,2048]{1,0:T(8,128)(2,1)} %get-tuple-element.40), channel_id=1, source_target_pairs={{0,32},{4,36},{8,40},{12,44},{16,48},{20,52},{24,56},{28,60},{32,6... | collective-permute-start | bytes 3145736 | tf_op jit(solution)/shard_map/ppermute | solution.py:32
  69.7 59.2 %collective-permute-start.10 = (bf16[256,2048]{1,0:T(8,128)(2,1)}, bf16[256,2048]{1,0:T(8,128)(2,1)S(1)}, u32[]{:S(2)}, u32[]{:S(2)}) collective-permute-start(bf16[256,2048]{1,0:T(8,128)(2,1)} %get-tuple-element.41), channel_id=1, source_target_pairs={{0,64},{4,68},{8,72},{12,76},{16,80},{20,84},{24,88},{28,92},{32,9... | collective-permute-start | bytes 3145736 | tf_op jit(solution)/shard_map/ppermute | solution.py:32
  71.7 57.2 %collective-permute-start.11 = (bf16[256,2048]{1,0:T(8,128)(2,1)}, bf16[256,2048]{1,0:T(8,128)(2,1)S(1)}, u32[]{:S(2)}, u32[]{:S(2)}) collective-permute-start(bf16[256,2048]{1,0:T(8,128)(2,1)} %get-tuple-element.42), channel_id=1, source_target_pairs={{0,96},{4,100},{8,104},{12,108},{16,112},{20,116},{24,120},{28,124... | collective-permute-start | bytes 3145736 | tf_op jit(solution)/shard_map/ppermute | solution.py:32
  128.9 1.0 copy-start.6
  129.0 1.3 copy-start.7
  129.0 1.7 copy-start.8
  152.6 98.8 %reduce-scatter.8.cloned.1.call-start = ((), (), s32[]{:S(2)}) async-start(), calls=%async_computation.9 | async-start | bytes 3932160 | tf_op jit(solution)/shard_map/reduce_scatter | solution.py:426
  153.3 6.5 %copy-start.12 = (f32[1024,1]{1,0:T(8,128)S(1)}, f32[1024,1]{1,0:T(8,128)}, u32[]{:S(2)}) copy-start(f32[1024,1]{1,0:T(8,128)} %get-tuple-element.51) | copy-start | bytes 12292
  153.3 53.6 %all-to-all-start.1 = ((bf16[4,256,2048]{2,1,0:T(8,128)(2,1)}), bf16[4,256,2048]{2,1,0:T(8,128)(2,1)}, u32[]{:S(2)}, u32[]{:S(2)}) async-start(bf16[4,256,2048]{2,1,0:T(8,128)(2,1)} %bitcast.77), calls=%async_computation.1 | async-start | bytes 8388608 | tf_op jit(solution)/shard_map/all_to_all | solution.py:386
  159.8 153.8 %reduce-scatter.6.cloned.1.call-start = ((), (), s32[]{:S(2)}) async-start(), calls=%async_computation.8 | async-start | bytes 3932160 | tf_op jit(solution)/shard_map/reduce_scatter | solution.py:429
  171.6 41.9 %collective-permute-start.12 = (bf16[256,2176]{1,0:T(8,128)(2,1)}, bf16[256,2176]{1,0:T(8,128)(2,1)S(1)}, u32[]{:S(2)}, u32[]{:S(2)}) collective-permute-start(bf16[256,2176]{1,0:T(8,128)(2,1)} %get-tuple-element.53), channel_id=1, source_target_pairs={{0,96},{4,100},{8,104},{12,108},{16,112},{20,116},{24,120},{28,124... | collective-permute-start | bytes 3342344 | tf_op jit(solution)/shard_map/ppermute | solution.py:32
  172.8 40.7 %collective-permute-start.13 = (bf16[256,2176]{1,0:T(8,128)(2,1)}, bf16[256,2176]{1,0:T(8,128)(2,1)S(1)}, u32[]{:S(2)}, u32[]{:S(2)}) collective-permute-start(bf16[256,2176]{1,0:T(8,128)(2,1)} %get-tuple-element.54), channel_id=1, source_target_pairs={{0,64},{4,68},{8,72},{12,76},{16,80},{20,84},{24,88},{28,92},{32,9... | collective-permute-start | bytes 3342344 | tf_op jit(solution)/shard_map/ppermute | solution.py:32
  173.8 49.6 %collective-permute-start.14 = (bf16[256,2176]{1,0:T(8,128)(2,1)}, bf16[256,2176]{1,0:T(8,128)(2,1)}, u32[]{:S(2)}, u32[]{:S(2)}) collective-permute-start(bf16[256,2176]{1,0:T(8,128)(2,1)} %get-tuple-element.55), channel_id=1, source_target_pairs={{0,32},{4,36},{8,40},{12,44},{16,48},{20,52},{24,56},{28,60},{32,6... | collective-permute-start | bytes 3342344 | tf_op jit(solution)/shard_map/ppermute | solution.py:32
  213.5 17.2 %collective-permute-start.7 = (bf16[512,2048]{1,0:T(8,128)(2,1)}, bf16[512,2048]{1,0:T(8,128)(2,1)}, u32[]{:S(2)}, u32[]{:S(2)}) collective-permute-start(bf16[512,2048]{1,0:T(8,128)(2,1)} %get-tuple-element.38), channel_id=1, source_target_pairs={{0,4},{4,0},{8,12},{12,8},{16,20},{20,16},{24,28},{28,24},{32,36},... | collective-permute-start | bytes 6291464 | tf_op jit(solution)/shard_map/ppermute | solution.py:32
  213.5 17.2 %copy-start.4 = (bf16[256,2176]{1,0:T(8,128)(2,1)}, bf16[256,2176]{1,0:T(8,128)(2,1)S(1)}, u32[]{:S(2)}) copy-start(bf16[256,2176]{1,0:T(8,128)(2,1)S(1)} %collective-permute-done.12.refs_9_) | copy-start | bytes 3342340
  213.6 9.8 %copy-start.5 = (bf16[256,2176]{1,0:T(8,128)(2,1)}, bf16[256,2176]{1,0:T(8,128)(2,1)S(1)}, u32[]{:S(2)}) copy-start(bf16[256,2176]{1,0:T(8,128)(2,1)S(1)} %collective-permute-done.13.refs_10_) | copy-start | bytes 3342340
  230.7 1.6 copy-start.3
  243.9 7.6 %collective-permute-start.15 = (bf16[512,2176]{1,0:T(8,128)(2,1)}, bf16[512,2176]{1,0:T(8,128)(2,1)}, u32[]{:S(2)}, u32[]{:S(2)}) collective-permute-start(bf16[512,2176]{1,0:T(8,128)(2,1)} %get-tuple-element.59), channel_id=1, source_target_pairs={{0,4},{4,0},{8,12},{12,8},{16,20},{20,16},{24,28},{28,24},{32,36},... | collective-permute-start | bytes 6684680 | tf_op jit(solution)/shard_map/ppermute | solution.py:32
  244.2 31.3 %all-to-all-start.2 = ((bf16[4,128,2048]{2,1,0:T(8,128)(2,1)}), bf16[4,128,2048]{2,1,0:T(8,128)(2,1)S(1)}, u32[]{:S(2)}, u32[]{:S(2)}) async-start(bf16[4,128,2048]{2,1,0:T(8,128)(2,1)} %bitcast.15), calls=%async_computation.2 | async-start | bytes 4194304 | tf_op jit(solution)/shard_map/all_to_all | solution.py:386
  247.9 44.6 %collective-permute-start.19 = (bf16[512,768]{1,0:T(8,128)(2,1)}, bf16[512,768]{1,0:T(8,128)(2,1)}, u32[]{:S(2)}, u32[]{:S(2)}) collective-permute-start(bf16[512,768]{1,0:T(8,128)(2,1)} %reduce-scatter.4.cloned.1.call-done), channel_id=1, source_target_pairs={{0,64},{4,68},{8,72},{12,76},{16,80},{20,84},{24,88},{28,92},{32,9... | collective-permute-start | bytes 2359304 | tf_op jit(solution)/shard_map/ppermute | solution.py:32
  251.3 57.5 %collective-permute-start.21 = (bf16[768,512]{1,0:T(8,128)(2,1)}, bf16[768,512]{1,0:T(8,128)(2,1)}, u32[]{:S(2)}, u32[]{:S(2)}) collective-permute-start(bf16[768,512]{1,0:T(8,128)(2,1)} %reduce-scatter.8.cloned.1.call-done), channel_id=1, source_target_pairs={{0,64},{4,68},{8,72},{12,76},{16,80},{20,84},{24,88},{28,92},{32,9... | collective-permute-start | bytes 2359304 | tf_op jit(solution)/shard_map/ppermute | solution.py:32
  254.3 5.9 %copy-start.15 = (s32[32]{0:T(128)S(1)}, s32[32]{0:T(128)}, u32[]{:S(2)}) copy-start(s32[32]{0:T(128)} %param.12) | copy-start | bytes 388
  255.6 55.7 %collective-permute-start.18 = (bf16[128,2176]{1,0:T(8,128)(2,1)}, bf16[128,2176]{1,0:T(8,128)(2,1)}, u32[]{:S(2)}, u32[]{:S(2)}) collective-permute-start(bf16[128,2176]{1,0:T(8,128)(2,1)} %get-tuple-element.71), channel_id=1, source_target_pairs={{0,8},{4,12},{8,16},{12,20},{16,24},{20,28},{24,0},{28,4},{32,40},... | collective-permute-start | bytes 1671176 | tf_op jit(solution)/shard_map/ppermute | solution.py:32
  257.0 55.0 %collective-permute-start.17 = (bf16[128,2176]{1,0:T(8,128)(2,1)}, bf16[128,2176]{1,0:T(8,128)(2,1)}, u32[]{:S(2)}, u32[]{:S(2)}) collective-permute-start(bf16[128,2176]{1,0:T(8,128)(2,1)} %get-tuple-element.72), channel_id=1, source_target_pairs={{0,16},{4,20},{8,24},{12,28},{16,0},{20,4},{24,8},{28,12},{32,48},... | collective-permute-start | bytes 1671176 | tf_op jit(solution)/shard_map/ppermute | solution.py:32
  257.6 55.2 %collective-permute-start.16 = (bf16[128,2176]{1,0:T(8,128)(2,1)}, bf16[128,2176]{1,0:T(8,128)(2,1)}, u32[]{:S(2)}, u32[]{:S(2)}) collective-permute-start(bf16[128,2176]{1,0:T(8,128)(2,1)} %get-tuple-element.73), channel_id=1, source_target_pairs={{0,24},{4,28},{8,0},{12,4},{16,8},{20,12},{24,16},{28,20},{32,56},... | collective-permute-start | bytes 1671176 | tf_op jit(solution)/shard_map/ppermute | solution.py:32
  276.8 38.8 %copy-start.14 = (s32[128,8]{0,1:T(8,128)S(1)}, s32[128,8]{0,1:T(8,128)}, u32[]{:S(2)}) copy-start(s32[128,8]{0,1:T(8,128)} %param.9) | copy-start | bytes 12292
  276.8 38.9 %copy-start.13 = (f32[128,8]{0,1:T(8,128)S(1)}, f32[128,8]{0,1:T(8,128)}, u32[]{:S(2)}) copy-start(f32[128,8]{0,1:T(8,128)} %param.10) | copy-start | bytes 12292
  313.6 20.8 %collective-permute-start.20 = (bf16[512,768]{1,0:T(8,128)(2,1)}, bf16[512,768]{1,0:T(8,128)(2,1)S(1)}, u32[]{:S(2)}, u32[]{:S(2)}) collective-permute-start(bf16[512,768]{1,0:T(8,128)(2,1)} %reduce-scatter.6.cloned.1.call-done), channel_id=1, source_target_pairs={{0,64},{4,68},{8,72},{12,76},{16,80},{20,84},{24,88},{28,92},{32,9... | collective-permute-start | bytes 2359304 | tf_op jit(solution)/shard_map/ppermute | solution.py:32
  319.7 14.7 %copy-start.9 = (bf16[512,768]{1,0:T(8,128)(2,1)S(1)}, bf16[512,768]{1,0:T(8,128)(2,1)}, u32[]{:S(2)}) copy-start(bf16[512,768]{1,0:T(8,128)(2,1)} %reduce-scatter.4.cloned.1.call-done) | copy-start | bytes 2359300
  319.7 14.7 %copy-start.10 = (bf16[512,768]{1,0:T(8,128)(2,1)S(1)}, bf16[512,768]{1,0:T(8,128)(2,1)}, u32[]{:S(2)}) copy-start(bf16[512,768]{1,0:T(8,128)(2,1)} %reduce-scatter.6.cloned.1.call-done) | copy-start | bytes 2359300
Sparse Core Ops, SparseCore 0:
  152.7 34.1 reduce-scatter.3
  189.2 37.9 reduce-scatter.7
  230.9 36.7 reduce-scatter.5
